TPU v7x, 128 devices: a whole 4x4x4 slice. The times are simulated.
128 devices in a mesh: section: 8 (over y_hi, z), dp: 16 (over y_lo, x, core).
Axes of the slice: x: 4, y: 4 (y_hi: 2, y_lo: 2; y = y_hi * 2 + y_lo), z: 4, core: 2. Of those that a mesh axis runs over, the one named last changes fastest.
Arguments:
- hidden_in: bfloat16 [12288, 1536], P('dp'), may hold values from -6 to 6
- segment_ids: int32 [48, 256], P('dp'), may hold values from 0 to 7, never falling along the last dimension, each value on 1 to 128 neighbouring positions
- cotangent: bfloat16 [12288, 1536], P('dp'), may hold values from -6 to 6
- in_proj: bfloat16 [8, 1536, 2304], P('section', 'dp'), may hold values from -1 to 1
- out_proj: bfloat16 [8, 768, 1536], P('section', 'dp'), may hold values from -0.21875 to 0.21875
- norm_gains: float32 [8, 1536], P('section'), may hold values from 0.5 to 1.5
Outputs:
- in_proj_grad: float32 [8, 1536, 2304], P('section', 'dp')
- out_proj_grad: float32 [8, 768, 1536], P('section', 'dp')
- gain_grad: float32 [8, 1536], P('section', 'dp')
- grad_rms: float32 [], replicated
Inputs may be any that keep to these rules, and one draw needn't show every extreme that they name: `segment_ids`: ids never fall along a row; at most 128 positions of a row share one id.
All inputs are finite; a program needn't handle non-finite values.
Results may differ from a plain program's by a relative error of at most 0.035.
Values may be sent and summed in bfloat16 or wider, within the bound.
No kernel may reach another device: no remote copies, remote signals or barrier semaphores. Data moves between devices by JAX's collectives and lax.ppermute only.
A program may use at most 128 MiB of HBM per device.

v0:
```python
import math

import jax
import jax.numpy as jnp
from jax import lax
from jax.sharding import PartitionSpec as P

HEAD_SIZE = 128


epsilon = 1e-05
masked_score = -1e30


def shifted(value, axis, steps):
    count = lax.axis_size(axis)
    leading, last = (max(0, -steps), min(count, count - steps))
    return lax.ppermute(value, axis, [(source, source + steps) for source in range(leading, last)])


def product(form, left, right):
    return jnp.einsum(form, left, right, preferred_element_type=jnp.float32)


def attend_parts(hidden, segments, in_weight, gains_row):
    batch_count, seq_length, feature_count = hidden.shape
    inner_width = in_weight.shape[1] // 3
    head_count = inner_width // HEAD_SIZE
    residual = hidden.astype(jnp.float32)
    inverse_rms = lax.rsqrt(jnp.mean(residual * residual, axis=-1, keepdims=True) + epsilon)
    unit_rows = residual * inverse_rms
    normed = (unit_rows * gains_row).astype(jnp.bfloat16)
    joined = jnp.dot(
        normed.reshape(-1, feature_count), in_weight, preferred_element_type=jnp.float32
    )
    joined = joined.astype(jnp.bfloat16).reshape(batch_count, seq_length, 3, head_count, HEAD_SIZE)
    query_rows = joined[:, :, 0]
    key_rows = joined[:, :, 1]
    value_rows = joined[:, :, 2]
    row_ids = lax.broadcasted_iota(jnp.int32, (seq_length, seq_length), 0)
    col_ids = lax.broadcasted_iota(jnp.int32, (seq_length, seq_length), 1)
    allowed = (col_ids <= row_ids)[None] & (segments[:, :, None] == segments[:, None, :])
    scores = product("bqhe,bkhe->bhqk", query_rows, key_rows) * HEAD_SIZE ** (-0.5)
    scores = jnp.where(allowed[:, None], scores, masked_score)
    row_max = jnp.max(scores, axis=-1, keepdims=True)
    exponentials = jnp.exp(scores - row_max)
    probabilities = exponentials / jnp.sum(exponentials, axis=-1, keepdims=True)
    weights_low = probabilities.astype(jnp.bfloat16)
    attended = product("bhqk,bkhe->bqhe", weights_low, value_rows).astype(jnp.bfloat16)
    attended = attended.reshape(batch_count, seq_length, inner_width)
    return (
        residual,
        inverse_rms,
        unit_rows,
        normed,
        query_rows,
        key_rows,
        value_rows,
        probabilities,
        weights_low,
        attended,
    )


def layer_forward(hidden, segments, in_weight, out_weight, gains_row):
    parts = attend_parts(hidden, segments, in_weight, gains_row)
    residual = parts[0]
    attended = parts[9]
    update = jnp.dot(
        attended.reshape(-1, attended.shape[-1]), out_weight, preferred_element_type=jnp.float32
    )
    return (residual + update.reshape(residual.shape)).astype(jnp.bfloat16)


def layer_backward(hidden, segments, grad_next, in_weight, out_weight, gains_row, groups):
    (
        residual,
        inverse_rms,
        unit_rows,
        normed,
        query_rows,
        key_rows,
        value_rows,
        probabilities,
        weights_low,
        attended,
    ) = attend_parts(hidden, segments, in_weight, gains_row)
    batch_count, seq_length, feature_count = hidden.shape
    inner_width = attended.shape[-1]
    head_count = inner_width // HEAD_SIZE
    out_grad = product("gtc,gtd->gcd", attended, grad_next)
    grad_attended = product("td,cd->tc", grad_next.reshape(-1, feature_count), out_weight)
    grad_attended = grad_attended.astype(jnp.bfloat16).reshape(
        batch_count, seq_length, head_count, HEAD_SIZE
    )
    grad_probs = product("bqhe,bkhe->bhqk", grad_attended, value_rows)
    grad_values = product("bhqk,bqhe->bkhe", weights_low, grad_attended)
    inner_sum = jnp.sum(grad_probs * probabilities, axis=-1, keepdims=True)
    grad_scores = (probabilities * (grad_probs - inner_sum) * HEAD_SIZE ** (-0.5)).astype(
        jnp.bfloat16
    )
    grad_queries = product("bhqk,bkhe->bqhe", grad_scores, key_rows)
    grad_keys = product("bhqk,bqhe->bkhe", grad_scores, query_rows)
    grad_joined = jnp.stack([grad_queries, grad_keys, grad_values], axis=2).astype(jnp.bfloat16)
    grad_joined = grad_joined.reshape(-1, 3 * inner_width)
    in_grad = product("gtd,gtc->gdc", normed, grad_joined.reshape(groups, -1, 3 * inner_width))
    grad_normed = product("tc,dc->td", grad_joined, in_weight).reshape(residual.shape)
    gain_grad = jnp.sum(grad_normed * unit_rows, axis=1)
    scaled = grad_normed * gains_row
    inner_mean = jnp.mean(scaled * unit_rows, axis=-1, keepdims=True)
    grad_in = (
        grad_next.astype(jnp.float32) + inverse_rms * (scaled - unit_rows * inner_mean)
    ).astype(jnp.bfloat16)
    return (grad_in, in_grad, out_grad, gain_grad)


def local(hidden_in, segment_ids, cotangent, in_proj, out_proj, norm_gains):
    section_index = lax.axis_index("section")
    section_count = lax.axis_size("section")
    micro_count = segment_ids.shape[0]
    seq_length = segment_ids.shape[1]
    feature_count = hidden_in.shape[1]
    gains_row = norm_gains[0]
    full_in, full_out = (
        lax.all_gather(in_proj[0], "dp", axis=0, tiled=True),
        lax.all_gather(out_proj[0], "dp", axis=0, tiled=True),
    )
    sequences = hidden_in.reshape(micro_count, seq_length, feature_count)
    loss_scale = 1.0 / math.sqrt(lax.axis_size("dp") * hidden_in.shape[0])
    seed_grads = (cotangent.astype(jnp.float32) * loss_scale).astype(jnp.bfloat16)
    seed_grads = seed_grads.reshape(micro_count, seq_length, feature_count)
    period_count = micro_count + section_count - 1

    def forward_period(period, received, stash):
        micro_index = period - section_index
        active = (micro_index >= 0) & (micro_index < micro_count)
        slot_index = jnp.clip(micro_index, 0, micro_count - 1)
        own_input = lax.dynamic_index_in_dim(sequences, slot_index, 0, keepdims=False)
        entering = jnp.where(section_index == 0, own_input, received)
        segments = lax.dynamic_index_in_dim(segment_ids, slot_index, 0, keepdims=True)
        leaving = lax.cond(
            active & (section_index < section_count - 1),
            lambda: layer_forward(entering[None], segments, full_in, full_out, gains_row)[0],
            lambda: jnp.zeros_like(entering),
        )
        kept_row = lax.dynamic_index_in_dim(stash, slot_index, 0, keepdims=False)
        stash = lax.dynamic_update_index_in_dim(
            stash, jnp.where(active, entering, kept_row), slot_index, 0
        )
        return (leaving, stash)

    leaving, stash = forward_period(0, jnp.zeros_like(sequences[0]), jnp.zeros_like(sequences))

    def forward_step(period, carried):
        previous, stash_now = carried
        received = shifted(previous, "section", 1)
        return forward_period(period, received, stash_now)

    leaving, stash = lax.fori_loop(1, period_count, forward_step, (leaving, stash))
    back_in, back_out = (
        lax.all_gather(in_proj[0], "dp", axis=0, tiled=True),
        lax.all_gather(out_proj[0], "dp", axis=0, tiled=True),
    )

    def backward_period(period, received, totals):
        micro_index = period - (section_count - 1 - section_index)
        active = (micro_index >= 0) & (micro_index < micro_count)
        slot_index = jnp.clip(micro_index, 0, micro_count - 1)
        seed_grad = lax.dynamic_index_in_dim(seed_grads, slot_index, 0, keepdims=False)
        arriving = jnp.where(section_index == section_count - 1, seed_grad, received)
        entering = lax.dynamic_index_in_dim(stash, slot_index, 0, keepdims=False)
        segments = lax.dynamic_index_in_dim(segment_ids, slot_index, 0, keepdims=True)

        def active_branch():
            grad_in, in_grad, out_grad, gain_grad = layer_backward(
                entering[None], segments, arriving[None], back_in, back_out, gains_row, 1
            )
            return (
                grad_in[0],
                (totals[0] + in_grad[0], totals[1] + out_grad[0], totals[2] + gain_grad[0]),
            )

        def spare_branch():
            return (jnp.zeros_like(arriving), totals)

        return lax.cond(active, active_branch, spare_branch)

    start_totals = (
        jnp.zeros(back_in.shape, jnp.float32),
        jnp.zeros(back_out.shape, jnp.float32),
        jnp.zeros((feature_count,), jnp.float32),
    )
    sending, totals = backward_period(0, jnp.zeros_like(sequences[0]), start_totals)

    def backward_step(period, carried):
        previous, totals_now = carried
        received = shifted(previous, "section", -1)
        return backward_period(period, received, totals_now)

    sending, totals = lax.fori_loop(1, period_count, backward_step, (sending, totals))
    in_sum, out_sum, gain_sum = (
        lax.psum_scatter(
            totals[0].astype(jnp.bfloat16), "dp", scatter_dimension=0, tiled=True
        ).astype(jnp.float32),
        lax.psum_scatter(
            totals[1].astype(jnp.bfloat16), "dp", scatter_dimension=0, tiled=True
        ).astype(jnp.float32),
        lax.psum_scatter(
            totals[2].astype(jnp.bfloat16), "dp", scatter_dimension=0, tiled=True
        ).astype(jnp.float32),
    )
    squares = jnp.sum(in_sum * in_sum) + jnp.sum(out_sum * out_sum) + jnp.sum(gain_sum * gain_sum)
    grand_total = lax.psum(squares, ("section", "dp"))
    entry_count = float(
        section_count * lax.axis_size("dp") * (in_sum.size + out_sum.size + gain_sum.size)
    )
    grad_rms = jnp.sqrt(grand_total / entry_count)
    return (in_sum[None], out_sum[None], gain_sum[None], grad_rms)


def solution(mesh):
    placed = (
        P("dp", None),
        P("dp", None),
        P("dp", None),
        P("section", "dp", None),
        P("section", "dp", None),
        P("section", None),
    )
    return jax.shard_map(
        local,
        mesh=mesh,
        in_specs=placed,
        out_specs=(P("section", "dp", None), P("section", "dp", None), P("section", "dp"), P()),
        check_vma=False,
    )
```

profile of v0, /device:TPU:2, one launch (start us, length us, event | category | flops | bytes accessed | tf_op | source)
XLA Modules:
  0.0 1351.6 jit_solution(17380691487536345634)
XLA Ops:
  12.8 33.2 %all-gather.7.cloned.1.call-done = bf16[1,768,1536]{2,1,0:T(8,128)(2,1)} async-done(((bf16[1,48,1536]{2,1,0:T(8,128)(2,1)}), bf16[1,768,1536]{2,1,0:T(8,128)(2,1)}) %all-gather.7.cloned.1.call-update) | async-done | bytes 2359312 | tf_op jit(solution)/shard_map/all_gather | solution.py:126
  46.0 48.1 %all-gather.5.cloned.1.call-done = bf16[1,1536,2304]{2,1,0:T(8,128)(2,1)} async-done(((bf16[1,96,2304]{2,1,0:T(8,128)(2,1)}), bf16[1,1536,2304]{2,1,0:T(8,128)(2,1)}) %all-gather.5.cloned.1.call-update) | async-done | bytes 7077904 | tf_op jit(solution)/shard_map/all_gather | solution.py:125
  95.0 17.9 %conditional.4 = (bf16[256,1536]{1,0:T(8,128)(2,1)}) conditional(s32[]{:T(128)} %convert_element_type.327, () %tuple.93, (pred[]{:T(512)}, bf16[1,256,1536]{2,1,0:T(8,128)(2,1)S(1)}, bf16[256,1536]{1,0:T(8,128)(2,1)}, f32[1,1536]{1,0:T(1,128)S(1)}, bf16[1536,2304]{1,0:T(8,128)(2,1)}, /*index=5*/s32[3,256]{1,0:T(4,128)}, s32[]{:T(128)}, ...), branch_computations={%region_0.1_spmd, %region_1.5_spmd} | conditional | flops 2726758656 | bytes 28546120 | solution.py:141
  96.2 6.4 convolution_convert_fusion
  112.9 285.6 %while.37 = (s32[]{:T(128)}, bf16[256,1536]{1,0:T(8,128)(2,1)}, bf16[3,256,1536]{2,1,0:T(8,128)(2,1)S(1)}, s32[]{:T(128)}, pred[]{:T(512)}, /*index=5*/pred[]{:T...) while((s32[]{:T(128)}, bf16[256,1536]{1,0:T(8,128)(2,1)}, ...), condition=%wide.region_11.12_spmd, body=%wide.region_5.11_spmd.sunk | while | flops 2727151872 | bytes 31167864 | solution.py:159
  114.3 17.6 %collective-permute-done = bf16[256,1536]{1,0:T(8,128)(2,1)S(1)} collective-permute-done((bf16[256,1536]{1,0:T(8,128)(2,1)}, bf16[256,1536]{1,0:T(8,128)(2,1)S(1)}, u32[]{:S(2)}, u32[]{:S(2)}) %collective-permute-start) | collective-permute-done | bytes 786464 | tf_op jit(solution)/shard_map/while/body/eval_jaxpr/ppermute | solution.py:18
  134.3 17.6 %conditional.8 = (bf16[256,1536]{1,0:T(8,128)(2,1)}) conditional(s32[]{:T(128)} %convert_element_type.513, () %tuple.129, (bf16[256,1536]{1,0:T(8,128)(2,1)S(1)}, f32[1,1536]{1,0:T(1,128)S(1)}, bf16[1536,2304]{1,0:T(8,128)(2,1)}, s32[3,256]{1,0:T(4,128)}, s32[]{:T(128)}, /*index=5*/bf16[768,1536]{1,0:T(8,128)(2,1)}) %tuple.130), branch_computations={%region_6.6_spmd, %region_7.10_spmd} | conditional | flops 2726365440 | bytes 19371052 | solution.py:141
  134.6 6.1 convolution_convert_fusion.2
  152.0 4.6 collective-permute-start
  156.6 16.9 %collective-permute-done = bf16[256,1536]{1,0:T(8,128)(2,1)S(1)} collective-permute-done((bf16[256,1536]{1,0:T(8,128)(2,1)}, bf16[256,1536]{1,0:T(8,128)(2,1)S(1)}, u32[]{:S(2)}, u32[]{:S(2)}) %collective-permute-start) | collective-permute-done | bytes 786464 | tf_op jit(solution)/shard_map/while/body/eval_jaxpr/ppermute | solution.py:18
  175.9 17.7 %conditional.8 = (bf16[256,1536]{1,0:T(8,128)(2,1)}) conditional(s32[]{:T(128)} %convert_element_type.513, () %tuple.129, (bf16[256,1536]{1,0:T(8,128)(2,1)S(1)}, f32[1,1536]{1,0:T(1,128)S(1)}, bf16[1536,2304]{1,0:T(8,128)(2,1)}, s32[3,256]{1,0:T(4,128)}, s32[]{:T(128)}, /*index=5*/bf16[768,1536]{1,0:T(8,128)(2,1)}) %tuple.130), branch_computations={%region_6.6_spmd, %region_7.10_spmd} | conditional | flops 2726365440 | bytes 19371052 | solution.py:141
  176.2 6.1 convolution_convert_fusion.2
  193.6 4.6 collective-permute-start
  198.2 16.0 %collective-permute-done = bf16[256,1536]{1,0:T(8,128)(2,1)S(1)} collective-permute-done((bf16[256,1536]{1,0:T(8,128)(2,1)}, bf16[256,1536]{1,0:T(8,128)(2,1)S(1)}, u32[]{:S(2)}, u32[]{:S(2)}) %collective-permute-start) | collective-permute-done | bytes 786464 | tf_op jit(solution)/shard_map/while/body/eval_jaxpr/ppermute | solution.py:18
  217.5 21.2 %collective-permute-start = (bf16[256,1536]{1,0:T(8,128)(2,1)}, bf16[256,1536]{1,0:T(8,128)(2,1)S(1)}, u32[]{:S(2)}, u32[]{:S(2)}) collective-permute-start(bf16[256,1536]{1,0:T(8,128)(2,1)} %get-tuple-element.1076), channel_id=1, source_target_pairs={{0,16},{16,32},{32,48},{48,64},{64,80},{80,96},{96,112},{1,17},{17... | collective-permute-start | bytes 2359304 | tf_op jit(solution)/shard_map/while/body/eval_jaxpr/ppermute | solution.py:18
  238.9 15.0 %collective-permute-done = bf16[256,1536]{1,0:T(8,128)(2,1)S(1)} collective-permute-done((bf16[256,1536]{1,0:T(8,128)(2,1)}, bf16[256,1536]{1,0:T(8,128)(2,1)S(1)}, u32[]{:S(2)}, u32[]{:S(2)}) %collective-permute-start) | collective-permute-done | bytes 786464 | tf_op jit(solution)/shard_map/while/body/eval_jaxpr/ppermute | solution.py:18
  257.3 4.6 collective-permute-start
  261.9 14.1 %collective-permute-done = bf16[256,1536]{1,0:T(8,128)(2,1)S(1)} collective-permute-done((bf16[256,1536]{1,0:T(8,128)(2,1)}, bf16[256,1536]{1,0:T(8,128)(2,1)S(1)}, u32[]{:S(2)}, u32[]{:S(2)}) %collective-permute-start) | collective-permute-done | bytes 786464 | tf_op jit(solution)/shard_map/while/body/eval_jaxpr/ppermute | solution.py:18
  279.4 20.1 %collective-permute-start = (bf16[256,1536]{1,0:T(8,128)(2,1)}, bf16[256,1536]{1,0:T(8,128)(2,1)S(1)}, u32[]{:S(2)}, u32[]{:S(2)}) collective-permute-start(bf16[256,1536]{1,0:T(8,128)(2,1)} %get-tuple-element.1076), channel_id=1, source_target_pairs={{0,16},{16,32},{32,48},{48,64},{64,80},{80,96},{96,112},{1,17},{17... | collective-permute-start | bytes 2359304 | tf_op jit(solution)/shard_map/while/body/eval_jaxpr/ppermute | solution.py:18
  299.6 13.5 %collective-permute-done = bf16[256,1536]{1,0:T(8,128)(2,1)S(1)} collective-permute-done((bf16[256,1536]{1,0:T(8,128)(2,1)}, bf16[256,1536]{1,0:T(8,128)(2,1)S(1)}, u32[]{:S(2)}, u32[]{:S(2)}) %collective-permute-start) | collective-permute-done | bytes 786464 | tf_op jit(solution)/shard_map/while/body/eval_jaxpr/ppermute | solution.py:18
  316.5 4.6 collective-permute-start
  321.2 12.6 collective-permute-done
  337.2 22.6 %collective-permute-start = (bf16[256,1536]{1,0:T(8,128)(2,1)}, bf16[256,1536]{1,0:T(8,128)(2,1)S(1)}, u32[]{:S(2)}, u32[]{:S(2)}) collective-permute-start(bf16[256,1536]{1,0:T(8,128)(2,1)} %get-tuple-element.1076), channel_id=1, source_target_pairs={{0,16},{16,32},{32,48},{48,64},{64,80},{80,96},{96,112},{1,17},{17... | collective-permute-start | bytes 2359304 | tf_op jit(solution)/shard_map/while/body/eval_jaxpr/ppermute | solution.py:18
  359.9 12.2 collective-permute-done
  375.5 8.2 collective-permute-start
  383.8 11.3 collective-permute-done
  398.4 13.9 %conditional.5 = (bf16[256,1536]{1,0:T(8,128)(2,1)}, f32[1536,2304]{1,0:T(8,128)S(1)}, f32[768,1536]{1,0:T(8,128)}, f32[1536]{0:T(1024)}) conditional(s32[]{:T(128)} %convert_element_type.324, () %tuple.92, (pred[]{:T(512)}, s32[]{:T(128)}, bf16[3,256,1536]{2,1,0:T(8,128)(2,1)}, bf16[256,1536]{1,0:T(8,128)(2,1)}, ...), branch_computations={%region_12.13_spmd, %region_13.20_spmd} | conditional | flops 7269779456 | bytes 121776424 | solution.py:186
  412.4 5.0 copy-done
  417.4 717.4 %while.38 = (s32[]{:T(128)}, bf16[256,1536]{1,0:T(8,128)(2,1)}, f32[1536,2304]{1,0:T(8,128)}, f32[768,1536]{1,0:T(8,128)}, f32[1536]{0:T(1024)}, /*index=5*/s32[...) while((s32[]{:T(128)}, bf16[256,1536]{1,0:T(8,128)(2,1)}, ...), condition=%wide.region_29.30_spmd, body=%wide.region_20.29_spmd.sunk | while | flops 7274499584 | bytes 146961056 | solution.py:200
  418.7 34.7 %collective-permute-done.1 = bf16[256,1536]{1,0:T(8,128)(2,1)S(1)} collective-permute-done((bf16[256,1536]{1,0:T(8,128)(2,1)}, bf16[256,1536]{1,0:T(8,128)(2,1)S(1)}, u32[]{:S(2)}, u32[]{:S(2)}) %collective-permute-start.1) | collective-permute-done | bytes 786464 | tf_op jit(solution)/shard_map/while/body/eval_jaxpr/ppermute | solution.py:18
  455.6 17.1 %collective-permute-done.1 = bf16[256,1536]{1,0:T(8,128)(2,1)S(1)} collective-permute-done((bf16[256,1536]{1,0:T(8,128)(2,1)}, bf16[256,1536]{1,0:T(8,128)(2,1)S(1)}, u32[]{:S(2)}, u32[]{:S(2)}) %collective-permute-start.1) | collective-permute-done | bytes 786464 | tf_op jit(solution)/shard_map/while/body/eval_jaxpr/ppermute | solution.py:18
  475.0 25.3 %collective-permute-done.1 = bf16[256,1536]{1,0:T(8,128)(2,1)S(1)} collective-permute-done((bf16[256,1536]{1,0:T(8,128)(2,1)}, bf16[256,1536]{1,0:T(8,128)(2,1)S(1)}, u32[]{:S(2)}, u32[]{:S(2)}) %collective-permute-start.1) | collective-permute-done | bytes 786464 | tf_op jit(solution)/shard_map/while/body/eval_jaxpr/ppermute | solution.py:18
  502.5 16.8 %collective-permute-done.1 = bf16[256,1536]{1,0:T(8,128)(2,1)S(1)} collective-permute-done((bf16[256,1536]{1,0:T(8,128)(2,1)}, bf16[256,1536]{1,0:T(8,128)(2,1)S(1)}, u32[]{:S(2)}, u32[]{:S(2)}) %collective-permute-start.1) | collective-permute-done | bytes 786464 | tf_op jit(solution)/shard_map/while/body/eval_jaxpr/ppermute | solution.py:18
  521.5 26.4 %collective-permute-done.1 = bf16[256,1536]{1,0:T(8,128)(2,1)S(1)} collective-permute-done((bf16[256,1536]{1,0:T(8,128)(2,1)}, bf16[256,1536]{1,0:T(8,128)(2,1)S(1)}, u32[]{:S(2)}, u32[]{:S(2)}) %collective-permute-start.1) | collective-permute-done | bytes 786464 | tf_op jit(solution)/shard_map/while/body/eval_jaxpr/ppermute | solution.py:18
  550.2 14.9 %collective-permute-done.1 = bf16[256,1536]{1,0:T(8,128)(2,1)S(1)} collective-permute-done((bf16[256,1536]{1,0:T(8,128)(2,1)}, bf16[256,1536]{1,0:T(8,128)(2,1)S(1)}, u32[]{:S(2)}, u32[]{:S(2)}) %collective-permute-start.1) | collective-permute-done | bytes 786464 | tf_op jit(solution)/shard_map/while/body/eval_jaxpr/ppermute | solution.py:18
  567.4 364.9 %collective-permute-done.1 = bf16[256,1536]{1,0:T(8,128)(2,1)S(1)} collective-permute-done((bf16[256,1536]{1,0:T(8,128)(2,1)}, bf16[256,1536]{1,0:T(8,128)(2,1)S(1)}, u32[]{:S(2)}, u32[]{:S(2)}) %collective-permute-start.1) | collective-permute-done | bytes 786464 | tf_op jit(solution)/shard_map/while/body/eval_jaxpr/ppermute | solution.py:18
  932.3 55.6 %conditional.9 = (bf16[256,1536]{1,0:T(8,128)(2,1)}, f32[1536,2304]{1,0:T(8,128)}, f32[768,1536]{1,0:T(8,128)}, f32[1536]{0:T(1024)}) conditional(s32[]{:T(128)} %convert_element_type.514, (f32[1536,2304]{1,0:T(8,128)}, f32[768,1536]{1,0:T(8,128)}, f32[1536]{0:T(1024)}) %tuple.132, (pred[]{:T(512)}, s32[]{:T(128)}, ...), branch_computations={%region_21.21_spmd, %region_22.28_spmd} | conditional | flops 7274499584 | bytes 143814976 | solution.py:186
  933.1 5.1 convolution_convert_fusion.7
  948.6 3.6 fusion.162
  952.1 4.3 fusion.127
  956.4 4.3 fusion.130
  963.4 12.4 convolution_add_fusion.2
  977.3 5.5 convolution_add_fusion.3
  989.2 16.4 %collective-permute-done.1 = bf16[256,1536]{1,0:T(8,128)(2,1)S(1)} collective-permute-done((bf16[256,1536]{1,0:T(8,128)(2,1)}, bf16[256,1536]{1,0:T(8,128)(2,1)S(1)}, u32[]{:S(2)}, u32[]{:S(2)}) %collective-permute-start.1) | collective-permute-done | bytes 786464 | tf_op jit(solution)/shard_map/while/body/eval_jaxpr/ppermute | solution.py:18
  1005.6 55.6 %conditional.9 = (bf16[256,1536]{1,0:T(8,128)(2,1)}, f32[1536,2304]{1,0:T(8,128)}, f32[768,1536]{1,0:T(8,128)}, f32[1536]{0:T(1024)}) conditional(s32[]{:T(128)} %convert_element_type.514, (f32[1536,2304]{1,0:T(8,128)}, f32[768,1536]{1,0:T(8,128)}, f32[1536]{0:T(1024)}) %tuple.132, (pred[]{:T(512)}, s32[]{:T(128)}, ...), branch_computations={%region_21.21_spmd, %region_22.28_spmd} | conditional | flops 7274499584 | bytes 143814976 | solution.py:186
  1006.5 5.1 convolution_convert_fusion.7
  1021.9 3.6 fusion.162
  1025.5 4.3 fusion.127
  1029.8 4.3 fusion.130
  1036.7 12.4 convolution_add_fusion.2
  1050.6 5.5 convolution_add_fusion.3
  1062.5 16.4 %collective-permute-done.1 = bf16[256,1536]{1,0:T(8,128)(2,1)S(1)} collective-permute-done((bf16[256,1536]{1,0:T(8,128)(2,1)}, bf16[256,1536]{1,0:T(8,128)(2,1)S(1)}, u32[]{:S(2)}, u32[]{:S(2)}) %collective-permute-start.1) | collective-permute-done | bytes 786464 | tf_op jit(solution)/shard_map/while/body/eval_jaxpr/ppermute | solution.py:18
  1078.9 55.6 %conditional.9 = (bf16[256,1536]{1,0:T(8,128)(2,1)}, f32[1536,2304]{1,0:T(8,128)}, f32[768,1536]{1,0:T(8,128)}, f32[1536]{0:T(1024)}) conditional(s32[]{:T(128)} %convert_element_type.514, (f32[1536,2304]{1,0:T(8,128)}, f32[768,1536]{1,0:T(8,128)}, f32[1536]{0:T(1024)}) %tuple.132, (pred[]{:T(512)}, s32[]{:T(128)}, ...), branch_computations={%region_21.21_spmd, %region_22.28_spmd} | conditional | flops 7274499584 | bytes 143814976 | solution.py:186
  1079.8 5.1 convolution_convert_fusion.7
  1098.8 4.3 fusion.127
  1103.1 4.3 fusion.130
  1110.0 12.4 convolution_add_fusion.2
  1123.9 5.5 convolution_add_fusion.3
  1134.8 4.0 convert_element_type.330
  1138.9 8.5 convert_element_type.328
  1150.0 23.4 %all-reduce = bf16[1536]{0:T(1024)(128)(2,1)S(1)} all-reduce(bf16[1536]{0:T(1024)(128)(2,1)S(1)} %convert_element_type.332), channel_id=6, replica_groups=mesh['section'=8,'dp'=16] {'dp'}, use_global_device_ids=true, to_apply=%region_32.33.clone | all-reduce | flops 1536 | bytes 6144
  1174.7 21.2 %reduce-scatter.5.cloned.1.call-done = bf16[48,1536]{1,0:T(8,128)(2,1)} async-done(((bf16[768,1536]{1,0:T(8,128)(2,1)}), bf16[48,1536]{1,0:T(8,128)(2,1)}) %reduce-scatter.5.cloned.1.call-update) | async-done | bytes 147472 | tf_op jit(solution)/shard_map/reduce_scatter | solution.py:205
  1197.5 71.0 %reduce-scatter.3.cloned.1.call-done = bf16[96,2304]{1,0:T(8,128)(2,1)} async-done(((bf16[1536,2304]{1,0:T(8,128)(2,1)}), bf16[96,2304]{1,0:T(8,128)(2,1)}) %reduce-scatter.3.cloned.1.call-update) | async-done | bytes 442384 | tf_op jit(solution)/shard_map/reduce_scatter | solution.py:202
  1274.0 66.9 %psum.7 = f32[]{:T(128)} all-reduce(f32[]{:T(128)S(6)} %add.153), channel_id=1, replica_groups=mesh['section'=8,'dp'=16] {'section','dp'}, use_global_device_ids=true, to_apply=%region_36.37 | all-reduce | flops 1 | bytes 8 | tf_op jit(solution)/shard_map/psum | solution.py:213
  (247 shorter events, 180.6 us)
Async XLA Ops:
  7.2 38.8 %all-gather.7.cloned.1.call-start = ((), (), s32[]{:S(2)}) async-start(), calls=%async_computation.5 | async-start | bytes 2506752 | tf_op jit(solution)/shard_map/all_gather | solution.py:126
  7.9 86.2 %all-gather.5.cloned.1.call-start = ((), (), s32[]{:S(2)}) async-start(), calls=%async_computation.4 | async-start | bytes 7520256 | tf_op jit(solution)/shard_map/all_gather | solution.py:125
  8.6 1187.3 %reduce-scatter.5.cloned.1.call-start = ((), (), s32[]{:S(2)}) async-start(), calls=%async_computation.3 | async-start | bytes 2506752 | tf_op jit(solution)/shard_map/reduce_scatter | solution.py:205
  8.9 1.9 copy-start.8
  10.8 84.2 %copy-start.11 = (f32[1,1536]{1,0:T(1,128)S(1)}, f32[1,1536]{1,0:T(1,128)}, u32[]{:S(2)}) copy-start(f32[1,1536]{1,0:T(1,128)} %param.23) | copy-start | bytes 18436
  104.2 1.5 copy-start.10
  107.2 2.3 copy-start.7
  112.9 19.1 %collective-permute-start = (bf16[256,1536]{1,0:T(8,128)(2,1)}, bf16[256,1536]{1,0:T(8,128)(2,1)S(1)}, u32[]{:S(2)}, u32[]{:S(2)}) collective-permute-start(bf16[256,1536]{1,0:T(8,128)(2,1)} %get-tuple-element.1076), channel_id=1, source_target_pairs={{0,16},{16,32},{32,48},{48,64},{64,80},{80,96},{96,112},{1,17},{17... | collective-permute-start | bytes 2359304 | tf_op jit(solution)/shard_map/while/body/eval_jaxpr/ppermute | solution.py:18
  131.9 0.9 copy-start.4
  152.0 21.5 %collective-permute-start = (bf16[256,1536]{1,0:T(8,128)(2,1)}, bf16[256,1536]{1,0:T(8,128)(2,1)S(1)}, u32[]{:S(2)}, u32[]{:S(2)}) collective-permute-start(bf16[256,1536]{1,0:T(8,128)(2,1)} %get-tuple-element.1076), channel_id=1, source_target_pairs={{0,16},{16,32},{32,48},{48,64},{64,80},{80,96},{96,112},{1,17},{17... | collective-permute-start | bytes 2359304 | tf_op jit(solution)/shard_map/while/body/eval_jaxpr/ppermute | solution.py:18
  173.5 0.9 copy-start.4
  193.6 20.6 %collective-permute-start = (bf16[256,1536]{1,0:T(8,128)(2,1)}, bf16[256,1536]{1,0:T(8,128)(2,1)S(1)}, u32[]{:S(2)}, u32[]{:S(2)}) collective-permute-start(bf16[256,1536]{1,0:T(8,128)(2,1)} %get-tuple-element.1076), channel_id=1, source_target_pairs={{0,16},{16,32},{32,48},{48,64},{64,80},{80,96},{96,112},{1,17},{17... | collective-permute-start | bytes 2359304 | tf_op jit(solution)/shard_map/while/body/eval_jaxpr/ppermute | solution.py:18
  214.2 0.9 copy-start.4
  217.5 36.4 %collective-permute-start = (bf16[256,1536]{1,0:T(8,128)(2,1)}, bf16[256,1536]{1,0:T(8,128)(2,1)S(1)}, u32[]{:S(2)}, u32[]{:S(2)}) collective-permute-start(bf16[256,1536]{1,0:T(8,128)(2,1)} %get-tuple-element.1076), channel_id=1, source_target_pairs={{0,16},{16,32},{32,48},{48,64},{64,80},{80,96},{96,112},{1,17},{17... | collective-permute-start | bytes 2359304 | tf_op jit(solution)/shard_map/while/body/eval_jaxpr/ppermute | solution.py:18
  253.9 0.9 copy-start.4
  257.3 18.8 %collective-permute-start = (bf16[256,1536]{1,0:T(8,128)(2,1)}, bf16[256,1536]{1,0:T(8,128)(2,1)S(1)}, u32[]{:S(2)}, u32[]{:S(2)}) collective-permute-start(bf16[256,1536]{1,0:T(8,128)(2,1)} %get-tuple-element.1076), channel_id=1, source_target_pairs={{0,16},{16,32},{32,48},{48,64},{64,80},{80,96},{96,112},{1,17},{17... | collective-permute-start | bytes 2359304 | tf_op jit(solution)/shard_map/while/body/eval_jaxpr/ppermute | solution.py:18
  276.1 0.9 copy-start.4
  279.4 33.8 %collective-permute-start = (bf16[256,1536]{1,0:T(8,128)(2,1)}, bf16[256,1536]{1,0:T(8,128)(2,1)S(1)}, u32[]{:S(2)}, u32[]{:S(2)}) collective-permute-start(bf16[256,1536]{1,0:T(8,128)(2,1)} %get-tuple-element.1076), channel_id=1, source_target_pairs={{0,16},{16,32},{32,48},{48,64},{64,80},{80,96},{96,112},{1,17},{17... | collective-permute-start | bytes 2359304 | tf_op jit(solution)/shard_map/while/body/eval_jaxpr/ppermute | solution.py:18
  313.2 0.9 copy-start.4
  316.5 17.2 %collective-permute-start = (bf16[256,1536]{1,0:T(8,128)(2,1)}, bf16[256,1536]{1,0:T(8,128)(2,1)S(1)}, u32[]{:S(2)}, u32[]{:S(2)}) collective-permute-start(bf16[256,1536]{1,0:T(8,128)(2,1)} %get-tuple-element.1076), channel_id=1, source_target_pairs={{0,16},{16,32},{32,48},{48,64},{64,80},{80,96},{96,112},{1,17},{17... | collective-permute-start | bytes 2359304 | tf_op jit(solution)/shard_map/while/body/eval_jaxpr/ppermute | solution.py:18
  333.8 0.9 copy-start.4
  337.2 35.0 %collective-permute-start = (bf16[256,1536]{1,0:T(8,128)(2,1)}, bf16[256,1536]{1,0:T(8,128)(2,1)S(1)}, u32[]{:S(2)}, u32[]{:S(2)}) collective-permute-start(bf16[256,1536]{1,0:T(8,128)(2,1)} %get-tuple-element.1076), channel_id=1, source_target_pairs={{0,16},{16,32},{32,48},{48,64},{64,80},{80,96},{96,112},{1,17},{17... | collective-permute-start | bytes 2359304 | tf_op jit(solution)/shard_map/while/body/eval_jaxpr/ppermute | solution.py:18
  372.1 0.9 copy-start.4
  375.5 19.6 %collective-permute-start = (bf16[256,1536]{1,0:T(8,128)(2,1)}, bf16[256,1536]{1,0:T(8,128)(2,1)S(1)}, u32[]{:S(2)}, u32[]{:S(2)}) collective-permute-start(bf16[256,1536]{1,0:T(8,128)(2,1)} %get-tuple-element.1076), channel_id=1, source_target_pairs={{0,16},{16,32},{32,48},{48,64},{64,80},{80,96},{96,112},{1,17},{17... | collective-permute-start | bytes 2359304 | tf_op jit(solution)/shard_map/while/body/eval_jaxpr/ppermute | solution.py:18
  395.1 0.9 copy-start.4
  412.4 5.1 copy-start
  417.4 36.0 %collective-permute-start.1 = (bf16[256,1536]{1,0:T(8,128)(2,1)}, bf16[256,1536]{1,0:T(8,128)(2,1)S(1)}, u32[]{:S(2)}, u32[]{:S(2)}) collective-permute-start(bf16[256,1536]{1,0:T(8,128)(2,1)} %get-tuple-element.1130), channel_id=1, source_target_pairs={{16,0},{32,16},{48,32},{64,48},{80,64},{96,80},{112,96},{17,1},{33... | collective-permute-start | bytes 2359304 | tf_op jit(solution)/shard_map/while/body/eval_jaxpr/ppermute | solution.py:18
  454.3 18.4 %collective-permute-start.1 = (bf16[256,1536]{1,0:T(8,128)(2,1)}, bf16[256,1536]{1,0:T(8,128)(2,1)S(1)}, u32[]{:S(2)}, u32[]{:S(2)}) collective-permute-start(bf16[256,1536]{1,0:T(8,128)(2,1)} %get-tuple-element.1130), channel_id=1, source_target_pairs={{16,0},{32,16},{48,32},{64,48},{80,64},{96,80},{112,96},{17,1},{33... | collective-permute-start | bytes 2359304 | tf_op jit(solution)/shard_map/while/body/eval_jaxpr/ppermute | solution.py:18
  473.7 26.6 %collective-permute-start.1 = (bf16[256,1536]{1,0:T(8,128)(2,1)}, bf16[256,1536]{1,0:T(8,128)(2,1)S(1)}, u32[]{:S(2)}, u32[]{:S(2)}) collective-permute-start(bf16[256,1536]{1,0:T(8,128)(2,1)} %get-tuple-element.1130), channel_id=1, source_target_pairs={{16,0},{32,16},{48,32},{64,48},{80,64},{96,80},{112,96},{17,1},{33... | collective-permute-start | bytes 2359304 | tf_op jit(solution)/shard_map/while/body/eval_jaxpr/ppermute | solution.py:18
  501.2 18.1 %collective-permute-start.1 = (bf16[256,1536]{1,0:T(8,128)(2,1)}, bf16[256,1536]{1,0:T(8,128)(2,1)S(1)}, u32[]{:S(2)}, u32[]{:S(2)}) collective-permute-start(bf16[256,1536]{1,0:T(8,128)(2,1)} %get-tuple-element.1130), channel_id=1, source_target_pairs={{16,0},{32,16},{48,32},{64,48},{80,64},{96,80},{112,96},{17,1},{33... | collective-permute-start | bytes 2359304 | tf_op jit(solution)/shard_map/while/body/eval_jaxpr/ppermute | solution.py:18
  520.2 27.7 %collective-permute-start.1 = (bf16[256,1536]{1,0:T(8,128)(2,1)}, bf16[256,1536]{1,0:T(8,128)(2,1)S(1)}, u32[]{:S(2)}, u32[]{:S(2)}) collective-permute-start(bf16[256,1536]{1,0:T(8,128)(2,1)} %get-tuple-element.1130), channel_id=1, source_target_pairs={{16,0},{32,16},{48,32},{64,48},{80,64},{96,80},{112,96},{17,1},{33... | collective-permute-start | bytes 2359304 | tf_op jit(solution)/shard_map/while/body/eval_jaxpr/ppermute | solution.py:18
  548.9 16.2 %collective-permute-start.1 = (bf16[256,1536]{1,0:T(8,128)(2,1)}, bf16[256,1536]{1,0:T(8,128)(2,1)S(1)}, u32[]{:S(2)}, u32[]{:S(2)}) collective-permute-start(bf16[256,1536]{1,0:T(8,128)(2,1)} %get-tuple-element.1130), channel_id=1, source_target_pairs={{16,0},{32,16},{48,32},{64,48},{80,64},{96,80},{112,96},{17,1},{33... | collective-permute-start | bytes 2359304 | tf_op jit(solution)/shard_map/while/body/eval_jaxpr/ppermute | solution.py:18
  566.1 366.2 %collective-permute-start.1 = (bf16[256,1536]{1,0:T(8,128)(2,1)}, bf16[256,1536]{1,0:T(8,128)(2,1)S(1)}, u32[]{:S(2)}, u32[]{:S(2)}) collective-permute-start(bf16[256,1536]{1,0:T(8,128)(2,1)} %get-tuple-element.1130), channel_id=1, source_target_pairs={{16,0},{32,16},{48,32},{64,48},{80,64},{96,80},{112,96},{17,1},{33... | collective-permute-start | bytes 2359304 | tf_op jit(solution)/shard_map/while/body/eval_jaxpr/ppermute | solution.py:18
  932.3 0.9 copy-start.3
  939.7 2.1 copy-start.2
  960.8 1.9 copy-start.5
  960.8 1.9 copy-start.6
  962.7 0.7 copy-start.12
  963.4 12.5 copy-start.17
  963.4 12.5 copy-start.19
  975.8 6.9 slice-start.2
  977.3 5.5 slice-start.3
  987.9 17.7 %collective-permute-start.1 = (bf16[256,1536]{1,0:T(8,128)(2,1)}, bf16[256,1536]{1,0:T(8,128)(2,1)S(1)}, u32[]{:S(2)}, u32[]{:S(2)}) collective-permute-start(bf16[256,1536]{1,0:T(8,128)(2,1)} %get-tuple-element.1130), channel_id=1, source_target_pairs={{16,0},{32,16},{48,32},{64,48},{80,64},{96,80},{112,96},{17,1},{33... | collective-permute-start | bytes 2359304 | tf_op jit(solution)/shard_map/while/body/eval_jaxpr/ppermute | solution.py:18
  1005.6 0.9 copy-start.3
  1013.0 2.1 copy-start.2
  1034.1 1.9 copy-start.5
  1034.1 1.9 copy-start.6
  1036.0 0.7 copy-start.12
  1036.7 12.5 copy-start.17
  1036.7 12.5 copy-start.19
  1049.2 6.9 slice-start.2
  1050.6 5.5 slice-start.3
  1061.2 17.7 %collective-permute-start.1 = (bf16[256,1536]{1,0:T(8,128)(2,1)}, bf16[256,1536]{1,0:T(8,128)(2,1)S(1)}, u32[]{:S(2)}, u32[]{:S(2)}) collective-permute-start(bf16[256,1536]{1,0:T(8,128)(2,1)} %get-tuple-element.1130), channel_id=1, source_target_pairs={{16,0},{32,16},{48,32},{64,48},{80,64},{96,80},{112,96},{17,1},{33... | collective-permute-start | bytes 2359304 | tf_op jit(solution)/shard_map/while/body/eval_jaxpr/ppermute | solution.py:18
  1078.9 0.9 copy-start.3
  1086.4 2.1 copy-start.2
  1107.4 1.9 copy-start.5
  1107.5 1.9 copy-start.6
  1109.4 0.7 copy-start.12
  1110.0 12.5 copy-start.17
  1110.0 12.5 copy-start.19
  1122.5 6.9 slice-start.2
  1123.9 5.5 slice-start.3
  1138.9 129.7 %reduce-scatter.3.cloned.1.call-start = ((), (), s32[]{:S(2)}) async-start(), calls=%async_computation.2 | async-start | bytes 7520256 | tf_op jit(solution)/shard_map/reduce_scatter | solution.py:202
  1147.4 0.7 copy-start.16
  (2 other events, 1.3 us)
Sparse Core Ops, SparseCore 0:
  9.7 36.2 all-gather.6
  47.7 46.3 all-gather.4
  1139.0 56.9 reduce-scatter.4
  1198.2 70.2 reduce-scatter.2
where the time goes:
time: 1370 us; the launch traced here: 1350 us
  waiting for transfers between devices  837 us (61%)
  matrix products  176 us (13%)
  starting transfers between devices  103 us (8%)
  blocking collectives  90.3 us (7%)
  other arithmetic  59.4 us (4%)
  local copies, waits for them, and re-layouts  56.9 us (4%)
  between operations  18.7 us (1%)
    ppermute x18, waiting for transfers between devices, shifted(): lax.ppermute(value, axis, [(source, source + steps) for source in range(l...  662 us
    dot_general x30, matrix products, product(): return jnp.einsum(form, left, right, preferred_element_type=jnp.float32)  116 us
    ppermute x18, starting transfers between devices, shifted(): lax.ppermute(value, axis, [(source, source + steps) for source in range(l...  103 us
    reduce_scatter x1, waiting for transfers between devices, local(): lax.psum_scatter(totals[0].astype(jnp.bfloat16), 'dp', scatter_dimension=...  71 us
    psum x1, blocking collectives, local(): grand_total = lax.psum(squares, ('section', 'dp'))  66.9 us
    all_gather x1, waiting for transfers between devices, local(): lax.all_gather(in_proj[0], 'dp', axis=0, tiled=True)  48.1 us
    dot_general x6, matrix products, attend_parts(): jnp.dot(normed.reshape(-1, feature_count), in_weight, preferred_element_t...  33.9 us
    all_gather x1, waiting for transfers between devices, local(): lax.all_gather(out_proj[0], 'dp', axis=0, tiled=True)  33.2 us
  transfers between devices with their start and end apart: 22, of which 22 were waited for; matrix products, arithmetic and copies ran while one was open for 1% of the time, Pallas kernels for 0%

commit v1 on v0

v1 whole, which is shorter than its diff:
```python
import functools
import math

import jax
import jax.numpy as jnp
from jax import lax
from jax.experimental import pallas as pl
from jax.experimental.pallas import tpu as pltpu
from jax.sharding import PartitionSpec as P

HEAD = 128
ROWS = 128
EPS = 1e-05
MASKED = -1e30
BF = jnp.bfloat16
F32 = jnp.float32


def mm(left, right, lc=1, rc=0):
    return lax.dot_general(left, right, (((lc,), (rc,)), ((), ())), preferred_element_type=F32)


def unit(h):
    r = lax.rsqrt(jnp.mean(h * h, axis=-1, keepdims=True) + EPS)
    return r, h * r


def weight_copies(pack, wi_s, wl_s, wr_s, sems, inner):
    half = wl_s.shape[1]
    third = 3 * inner
    wi = [
        pltpu.make_async_copy(
            pack.at[:, :, pl.ds(k * inner, inner)], wi_s.at[:, :, pl.ds(k * inner, inner)], sems.at[k]
        )
        for k in range(3)
    ]
    wo = [
        pltpu.make_async_copy(pack.at[:, pl.ds(0, half), pl.ds(third, inner)], wl_s, sems.at[3]),
        pltpu.make_async_copy(pack.at[:, pl.ds(half, half), pl.ds(third, inner)], wr_s, sems.at[4]),
    ]
    return wi, wo


def forward_kernel(cycle, micro, last, sec, recv, hid, bias, gains, pack, *refs):
    (sh, sa, sq, so, sl) = refs[5:10]
    out = refs[10]
    (h_s, wi_s, wl_s, wr_s, a_s, q_s, o_s, kv_s, b_s, l_s, n_s, sems) = refs[11:]
    inner = o_s.shape[1]
    feat = h_s.shape[1]
    heads = inner // HEAD
    odd = cycle % 2 == 1
    keys = 2 * ROWS if odd else ROWS
    section = sec[0]
    m = cycle - 2 * section

    @pl.when((m >= 0) & (m < micro))
    def _():
        from_in = pltpu.make_async_copy(hid.at[pl.ds(m * ROWS, ROWS)], h_s, sems.at[5])
        from_left = pltpu.make_async_copy(recv, h_s, sems.at[5])

        @pl.when(section == 0)
        def _():
            from_in.start()

        @pl.when(section != 0)
        def _():
            from_left.start()

        wi, wo = weight_copies(pack, wi_s, wl_s, wr_s, sems, inner)
        for copy in wi:
            copy.start()
        load_b = pltpu.make_async_copy(bias.at[pl.ds(m * ROWS, ROWS)], b_s, sems.at[6])
        load_b.start()
        if odd:
            load_kv = pltpu.make_async_copy(
                sq.at[m - 1, :, pl.ds(inner, 2 * inner)], kv_s, sems.at[7]
            )
            load_kv.start()
        for copy in wo:
            copy.start()
        from_left.wait()
        save_h = pltpu.make_async_copy(h_s, sh.at[m], sems.at[8])
        save_h.start()
        h = h_s[...].astype(F32)
        _, u = unit(h)
        a_s[...] = (u * gains[...]).astype(BF)
        save_a = pltpu.make_async_copy(a_s, sa.at[m], sems.at[9])
        save_a.start()
        a = a_s[...]
        for k in range(3):
            wi[k].wait()
            w = wi_s[:, :, k * inner:(k + 1) * inner].reshape(feat, inner)
            q_s[:, k * inner:(k + 1) * inner] = mm(a, w).astype(BF)
        save_q = pltpu.make_async_copy(q_s, sq.at[m], sems.at[10])
        save_q.start()
        load_b.wait()
        if odd:
            load_kv.wait()
        lane = lax.broadcasted_iota(jnp.int32, (ROWS, HEAD), 1)
        lse = jnp.zeros((ROWS, HEAD), F32)
        mask = b_s[:, :keys]
        for e in range(heads):
            lo, hi = e * HEAD, (e + 1) * HEAD
            q = q_s[:, lo:hi]
            k = q_s[:, inner + lo:inner + hi]
            v = q_s[:, 2 * inner + lo:2 * inner + hi]
            if odd:
                k = jnp.concatenate([kv_s[:, lo:hi], k], axis=0)
                v = jnp.concatenate([kv_s[:, inner + lo:inner + hi], v], axis=0)
            s = mm(q, k, 1, 1) * HEAD ** (-0.5) + mask
            top = jnp.max(s, axis=-1, keepdims=True)
            x = jnp.exp(s - top)
            total = jnp.sum(x, axis=-1, keepdims=True)
            p = x / total
            o_s[:, lo:hi] = mm(p.astype(BF), v).astype(BF)
            lse = jnp.where(lane == e, top + jnp.log(total), lse)
        l_s[...] = lse
        save_o = pltpu.make_async_copy(o_s, so.at[m], sems.at[11])
        save_o.start()
        save_l = pltpu.make_async_copy(l_s, sl.at[m], sems.at[12])
        save_l.start()
        for copy in wo:
            copy.wait()

        @pl.when(section != last)
        def _():
            o = o_s[...]
            for part, w in ((0, wl_s), (1, wr_s)):
                cols = slice(part * inner, (part + 1) * inner)
                n_s[:, cols] = (
                    h_s[:, cols].astype(F32) + mm(o, w[...].reshape(inner, inner))
                ).astype(BF)
            send = pltpu.make_async_copy(n_s, out, sems.at[13])
            send.start()
            send.wait()

        for copy in (save_h, save_a, save_q, save_o, save_l):
            copy.wait()


def backward_kernel(cycle, first, micro, last, sec, recv, seeds, bias, gains, pack, *refs):
    (sh, sa, sq, so, sl, sg, sd, sn, sp) = refs[9:18]
    out = refs[18]
    (h_s, wi_s, wl_s, wr_s, g_s, q_s, d_s, k_s, v_s, b_s, l_s, pd_s, gn_s, n_s, do_s, sems) = refs[19:]
    inner = k_s.shape[1]
    feat = h_s.shape[1]
    heads = inner // HEAD
    late = (cycle - first) % 2 == 0
    keys = 2 * ROWS if late else ROWS
    section = sec[0]
    n = cycle - first - 2 * (last - section)

    @pl.when((n >= 0) & (n < micro))
    def _():
        m = n + 1 if late else n - 1
        from_seed = pltpu.make_async_copy(seeds.at[pl.ds(m * ROWS, ROWS)], g_s, sems.at[5])
        from_right = pltpu.make_async_copy(recv, g_s, sems.at[5])

        @pl.when(section == last)
        def _():
            from_seed.start()

        @pl.when(section != last)
        def _():
            from_right.start()

        wi, wo = weight_copies(pack, wi_s, wl_s, wr_s, sems, inner)
        for copy in wo:
            copy.start()
        own = keys - ROWS
        loads = [
            pltpu.make_async_copy(sq.at[m, :, pl.ds(0, inner)], q_s, sems.at[6]),
            pltpu.make_async_copy(sq.at[m, :, pl.ds(inner, inner)], k_s.at[pl.ds(own, ROWS)], sems.at[7]),
            pltpu.make_async_copy(
                sq.at[m, :, pl.ds(2 * inner, inner)], v_s.at[pl.ds(own, ROWS)], sems.at[8]
            ),
            pltpu.make_async_copy(bias.at[pl.ds(m * ROWS, ROWS)], b_s, sems.at[9]),
            pltpu.make_async_copy(sl.at[m], l_s, sems.at[10]),
            pltpu.make_async_copy(sh.at[m], h_s, sems.at[11]),
        ]
        if late:
            loads.append(
                pltpu.make_async_copy(
                    sq.at[m - 1, :, pl.ds(inner, inner)], k_s.at[pl.ds(0, ROWS)], sems.at[12]
                )
            )
            loads.append(
                pltpu.make_async_copy(
                    sq.at[m - 1, :, pl.ds(2 * inner, inner)], v_s.at[pl.ds(0, ROWS)], sems.at[13]
                )
            )
        else:
            loads.append(pltpu.make_async_copy(sp, pd_s, sems.at[12]))
        for copy in loads:
            copy.start()
        for copy in wi:
            copy.start()
        from_right.wait()
        save_g = pltpu.make_async_copy(g_s, sg.at[m], sems.at[14])
        save_g.start()
        for copy in wo:
            copy.wait()
        do_s[...] = (
            mm(g_s[:, :inner], wl_s[...].reshape(inner, inner), 1, 1)
            + mm(g_s[:, inner:], wr_s[...].reshape(inner, inner), 1, 1)
        ).astype(BF)
        for copy in loads:
            copy.wait()
        mask = b_s[:, :keys]
        scale = HEAD ** (-0.5)
        for e in range(heads):
            lo, hi = e * HEAD, (e + 1) * HEAD
            q = q_s[:, lo:hi]
            k = k_s[:keys, lo:hi]
            v = v_s[:keys, lo:hi]
            do = do_s[:, lo:hi]
            s = mm(q, k, 1, 1) * scale + mask
            p = jnp.exp(s - l_s[:, e:e + 1])
            dp = mm(do, v, 1, 1)
            inside = jnp.sum(dp * p, axis=-1, keepdims=True)
            ds = (p * (dp - inside) * scale).astype(BF)
            d_s[:, lo:hi] = mm(ds, k).astype(BF)
            dk = mm(ds, q, 0, 0)
            dv = mm(p.astype(BF), do, 0, 0)
            if late:
                pd_s[:, lo:hi] = dk[:ROWS]
                pd_s[:, inner + lo:inner + hi] = dv[:ROWS]
                dk, dv = dk[ROWS:], dv[ROWS:]
            else:
                dk = dk + pd_s[:, lo:hi]
                dv = dv + pd_s[:, inner + lo:inner + hi]
            d_s[:, inner + lo:inner + hi] = dk.astype(BF)
            d_s[:, 2 * inner + lo:2 * inner + hi] = dv.astype(BF)
        saves = [save_g, pltpu.make_async_copy(d_s, sd.at[m], sems.at[15])]
        saves[-1].start()
        if late:
            saves.append(pltpu.make_async_copy(pd_s, sp, sems.at[16]))
            saves[-1].start()
        r, u = unit(h_s[...].astype(F32))
        da = None
        for k in range(3):
            wi[k].wait()
            cols = slice(k * inner, (k + 1) * inner)
            term = mm(d_s[:, cols], wi_s[:, :, cols].reshape(feat, inner), 1, 1)
            da = term if da is None else da + term
        gn_s[...] = jnp.sum((da * u).reshape(ROWS // 8, 8, feat), axis=0)
        saves.append(pltpu.make_async_copy(gn_s, sn.at[m], sems.at[17]))
        saves[-1].start()
        e = da * gains[...]
        mean = jnp.mean(e * u, axis=-1, keepdims=True)
        n_s[...] = (g_s[...].astype(F32) + r * (e - u * mean)).astype(BF)
        saves.append(pltpu.make_async_copy(n_s, out, sems.at[18]))
        saves[-1].start()
        for copy in saves:
            copy.wait()


ANY = pl.BlockSpec(memory_space=pl.ANY)
SMEM = pl.BlockSpec(memory_space=pltpu.SMEM)
VMEM = pl.BlockSpec(memory_space=pltpu.VMEM)


def call(body, ins, in_specs, states, out_shape, scratch, flops, name):
    count = len(ins)
    shapes = [jax.ShapeDtypeStruct(s.shape, s.dtype) for s in states]
    got = pl.pallas_call(
        body,
        out_shape=shapes + [out_shape],
        in_specs=in_specs + [ANY] * len(states),
        out_specs=[ANY] * (len(states) + 1),
        scratch_shapes=scratch,
        input_output_aliases={count + i: i for i in range(len(states))},
        compiler_params=pltpu.CompilerParams(vmem_limit_bytes=20 * 1024 * 1024),
        cost_estimate=pl.CostEstimate(flops=flops, bytes_accessed=12 * 1024 * 1024, transcendentals=0),
        name=name,
    )(*ins, *states)
    return got[-1], list(got[:-1])


def spread_sum(value, whole):
    rounds = [[1], [2, 4, 6], [8]]
    if whole:
        rounds = [[1], [2, 4, 6], [8, 64, 72], [16, 32, 48]]
    for masks in rounds:
        got = [
            lax.ppermute(value, ("section", "dp"), [(i, i ^ mask) for i in range(128)])
            for mask in masks
        ]
        for other in got:
            value = value + other
    return value


def local(hidden_in, segment_ids, cotangent, in_proj, out_proj, norm_gains):
    section = lax.axis_index("section")
    sections = lax.axis_size("section")
    width = lax.axis_size("dp")
    last = sections - 1
    seqs, length = segment_ids.shape
    feat = hidden_in.shape[1]
    shard = in_proj.shape[1]
    inner = out_proj.shape[1] * width
    micro = seqs * length // ROWS
    half = out_proj.shape[1]
    wo = jnp.concatenate([out_proj[0, :, :inner], out_proj[0, :, inner:]], axis=0)
    pack = lax.all_gather(jnp.concatenate([in_proj[0], wo], axis=1), "dp", axis=0)
    loss_scale = 1.0 / math.sqrt(width * hidden_in.shape[0])
    seeds = (cotangent.astype(F32) * loss_scale).astype(BF)
    rows = lax.broadcasted_iota(jnp.int32, (length, length), 0)
    cols = lax.broadcasted_iota(jnp.int32, (length, length), 1)
    allowed = (cols <= rows)[None] & (segment_ids[:, :, None] == segment_ids[:, None, :])
    bias = jnp.where(allowed, 0.0, MASKED).astype(F32).reshape(seqs * length, length)
    sec = jnp.full((1,), section, jnp.int32)

    def blank(*shape, dtype=BF):
        return jnp.zeros(shape, dtype)

    def vmem(*shape, dtype=BF):
        return pltpu.VMEM(shape, dtype)

    weights = [vmem(width, shard, 3 * inner), vmem(width, half, inner), vmem(width, half, inner)]
    f_scratch = (
        [vmem(ROWS, feat)] + weights
        + [vmem(ROWS, feat), vmem(ROWS, 3 * inner), vmem(ROWS, inner), vmem(ROWS, 2 * inner)]
        + [vmem(ROWS, length, dtype=F32), vmem(ROWS, HEAD, dtype=F32), vmem(ROWS, feat)]
        + [pltpu.SemaphoreType.DMA((14,))]
    )
    b_scratch = (
        [vmem(ROWS, feat)] + weights
        + [vmem(ROWS, feat), vmem(ROWS, inner), vmem(ROWS, 3 * inner)]
        + [vmem(2 * ROWS, inner), vmem(2 * ROWS, inner)]
        + [vmem(ROWS, length, dtype=F32), vmem(ROWS, HEAD, dtype=F32)]
        + [vmem(ROWS, 2 * inner, dtype=F32), vmem(8, feat, dtype=F32)]
        + [vmem(ROWS, feat), vmem(ROWS, inner)]
        + [pltpu.SemaphoreType.DMA((19,))]
    )
    states = [
        blank(micro, ROWS, feat),
        blank(micro, ROWS, feat),
        blank(micro, ROWS, 3 * inner),
        blank(micro, ROWS, inner),
        blank(micro, ROWS, HEAD, dtype=F32),
        blank(micro, ROWS, feat),
        blank(micro, ROWS, 3 * inner),
        blank(micro, 8, feat, dtype=F32),
        blank(ROWS, 2 * inner, dtype=F32),
    ]
    moved = jax.ShapeDtypeStruct((ROWS, feat), BF)
    per_row = 2 * feat * 4 * inner
    first = 2 * last + 1
    end = first + 2 * last + micro
    gains = norm_gains
    f_recv, b_recv = {}, {}
    for cycle in range(end):
        on = [s for s in range(sections) if 0 <= cycle - 2 * s < micro]
        if on:
            out, states[:5] = call(
                functools.partial(forward_kernel, cycle, micro, last),
                [sec, f_recv.get(cycle, hidden_in[:ROWS]), hidden_in, bias, gains, pack],
                [SMEM, ANY, ANY, ANY, VMEM, ANY],
                states[:5], moved, f_scratch, ROWS * per_row, "fwd_half",
            )
            pairs = [(s, s + 1) for s in on if s < last]
            if pairs:
                f_recv[cycle + 2] = lax.ppermute(out, "section", pairs)
        on = [s for s in range(sections) if 0 <= cycle - first - 2 * (last - s) < micro]
        if on:
            out, states = call(
                functools.partial(backward_kernel, cycle, first, micro, last),
                [sec, b_recv.get(cycle, seeds[:ROWS]), seeds, bias, gains, pack],
                [SMEM, ANY, ANY, ANY, VMEM, ANY],
                states, moved, b_scratch, 2 * ROWS * per_row, "bwd_half",
            )
            pairs = [(s, s - 1) for s in on if s > 0]
            if pairs:
                b_recv[cycle + 2] = lax.ppermute(out, "section", pairs)
    sa, so, sg, sd, sn = states[1], states[3], states[5], states[6], states[7]
    tokens = micro * ROWS
    out_part = mm(so.reshape(tokens, inner), sg.reshape(tokens, feat), 0, 0).astype(BF)
    in_part = mm(sa.reshape(tokens, feat), sd.reshape(tokens, 3 * inner), 0, 0).astype(BF)
    gain_part = jnp.sum(sn, axis=(0, 1)).astype(BF).astype(F32).reshape(feat // HEAD, HEAD)
    out_sum = lax.psum_scatter(out_part, "dp", scatter_dimension=0, tiled=True).astype(F32)
    in_sum = lax.psum_scatter(in_part, "dp", scatter_dimension=0, tiled=True).astype(F32)
    gain_all = spread_sum(gain_part, False).reshape(feat)
    own = feat // width
    gain_sum = lax.dynamic_slice_in_dim(gain_all, lax.axis_index("dp") * own, own)
    squares = jnp.sum(in_sum * in_sum) + jnp.sum(out_sum * out_sum) + jnp.sum(gain_sum * gain_sum)
    grand_total = spread_sum(jnp.full((8, HEAD), squares, F32), True)[0, 0]
    count = float(sections * width * (in_sum.size + out_sum.size + gain_sum.size))
    return (in_sum[None], out_sum[None], gain_sum[None], jnp.sqrt(grand_total / count))


def solution(mesh):
    placed = (
        P("dp", None),
        P("dp", None),
        P("dp", None),
        P("section", "dp", None),
        P("section", "dp", None),
        P("section", None),
    )
    return jax.shard_map(
        local,
        mesh=mesh,
        in_specs=placed,
        out_specs=(P("section", "dp", None), P("section", "dp", None), P("section", "dp"), P()),
        check_vma=False,
    )
```

time: 1370 us -> 726 us (0.53)
  waiting for transfers between devices: 837 us -> 240 us
  matrix products: 176 us -> 13.3 us
  Pallas kernels: 0 us -> 162 us
  starting transfers between devices: 103 us -> 260 us
  blocking collectives: 90.3 us -> 0 us
  other arithmetic: 59.4 us -> 10.9 us
  local copies, waits for them, and re-layouts: 56.9 us -> 11.7 us
    ppermute x18 -> x51, waiting for transfers between devices: 662 us -> 77.6 us  [the longest x18 56.7 us: local(): b_recv[cycle + 2] = lax.ppermute(out, 'section', pairs)]
    pallas_call x0 -> x40, Pallas kernels: none -> 162 us  [call(): pl.pallas_call(body, out_shape=shapes + [out_shape], in_specs=in_specs +...]
    ppermute x18 -> x51, starting transfers between devices: 103 us -> 260 us  [the longest x18 123 us: local(): b_recv[cycle + 2] = lax.ppermute(out, 'section', pairs)]
    dot_general x39 -> x2, matrix products: 160 us -> 13.3 us  [mm(): lax.dot_general(left, right, (((lc,), (rc,)), ((), ())), preferred_elemen...]
    psum x1 -> x0, blocking collectives: 66.9 us -> none  [local(): grand_total = lax.psum(squares, ('section', 'dp'))]
    all_gather x2 -> x1, waiting for transfers between devices: 81.2 us -> 57.5 us  [local(): lax.all_gather(jnp.concatenate([in_proj[0], wo], axis=1), 'dp', axis=0)]
    unnamed x1 -> x0, blocking collectives: 23.4 us -> none
    convert_element_type x10 -> x2, other arithmetic: 19.9 us -> 0.47 us  [the longest x1 0.47 us: local(): seeds = (cotangent.astype(F32) * loss_scale).astype(BF)]
  transfers between devices with their start and end apart: 22 -> 54, of which waited for: 22 -> 21; matrix products, arithmetic and copies ran while one was open for 1% -> 3% of each run, Pallas kernels for 0% -> 20%
where the time goes in v1:
time: 726 us; the launch traced here: 717 us
  starting transfers between devices  260 us (36%)
  waiting for transfers between devices  240 us (33%)
  Pallas kernels  162 us (22%)
  between operations  19 us (3%)
  matrix products  13.3 us (2%)
  local copies, waits for them, and re-layouts  11.7 us (2%)
  other arithmetic  10.9 us (2%)
    pallas_call x40, Pallas kernels, call(): pl.pallas_call(body, out_shape=shapes + [out_shape], in_specs=in_specs +...  162 us
    ppermute x18, starting transfers between devices, local(): b_recv[cycle + 2] = lax.ppermute(out, 'section', pairs)  123 us
    ppermute x18, starting transfers between devices, local(): f_recv[cycle + 2] = lax.ppermute(out, 'section', pairs)  82.5 us
    reduce_scatter x1, waiting for transfers between devices, local(): lax.psum_scatter(in_part, 'dp', scatter_dimension=0, tiled=True).astype(F32)  71 us
    all_gather x1, waiting for transfers between devices, local(): lax.all_gather(jnp.concatenate([in_proj[0], wo], axis=1), 'dp', axis=0)  57.5 us
    ppermute x18, waiting for transfers between devices, local(): b_recv[cycle + 2] = lax.ppermute(out, 'section', pairs)  56.7 us
    ppermute x15, starting transfers between devices, spread_sum(): lax.ppermute(value, ('section', 'dp'), [(i, i ^ mask) for i in range(128)])  54.6 us
    reduce_scatter x1, waiting for transfers between devices, local(): lax.psum_scatter(out_part, 'dp', scatter_dimension=0, tiled=True)  34.1 us
  transfers between devices with their start and end apart: 54, of which 21 were waited for; matrix products, arithmetic and copies ran while one was open for 3% of the time, Pallas kernels for 20%

profile of v1, /device:TPU:2, one launch (start us, length us, event | category | flops | bytes accessed | tf_op | source)
XLA Modules:
  0.0 717.0 jit_solution(14833381757552988486)
XLA Ops:
  8.2 1.9 maximum_maximum_fusion
  12.1 57.5 %all-gather.3.cloned.1.call-done = bf16[1536,3072]{1,0:T(8,128)(2,1)} async-done(((bf16[96,3072]{1,0:T(8,128)(2,1)}), bf16[1536,3072]{1,0:T(8,128)(2,1)}) %all-gather.3.cloned.1.call-update) | async-done | bytes 9437200 | tf_op jit(solution)/shard_map/all_gather | solution.py:306
  70.4 2.9 copy-done
  73.3 1.7 copy-done.2
  75.0 7.0 fwd_half.20
  81.9 1.3 collective-permute-start
  83.3 6.5 fwd_half.21
  89.8 1.3 collective-permute-start.2
  91.1 1.5 collective-permute-done.recv
  92.7 7.0 fwd_half.22
  99.6 4.4 collective-permute-start.1
  104.0 7.8 %fwd_half.23 = (bf16[6,128,1536]{2,1,0:T(8,128)(2,1)S(1)}, bf16[6,128,1536]{2,1,0:T(8,128)(2,1)S(1)}, bf16[6,128,2304]{2,1,0:T(8,128)(2,1)S(1)}, bf16[6,128,768]...) custom-call(s32[1]{0:T(128)} %bitcast.sec, ...), custom_call_target="tpu_custom_call", output_to_operand_aliasing={{0}: (6, {}), {1}: (7, {}), {2}: (8, {}), {3}: (9, {}), {4}... | custom-call | flops 1207959552 | bytes 12582912 | tf_op jit(solution)/shard_map/fwd_half/pallas_call | solution.py:266
  111.8 1.9 collective-permute-start.4
  113.8 7.0 fwd_half.24
  120.8 2.5 collective-permute-start.3
  123.3 6.5 fwd_half.25
  129.8 2.7 collective-permute-start.6
  133.4 6.1 collective-permute-done.6.recv
  139.5 7.6 %fwd_half.27 = (bf16[6,128,1536]{2,1,0:T(8,128)(2,1)S(1)}, bf16[6,128,1536]{2,1,0:T(8,128)(2,1)S(1)}, bf16[6,128,2304]{2,1,0:T(8,128)(2,1)S(1)}, bf16[6,128,768]...) custom-call(s32[1]{0:T(128)} %bitcast.sec, ...), custom_call_target="tpu_custom_call", output_to_operand_aliasing={{0}: (6, {}), {1}: (7, {}), {2}: (8, {}), {3}: (9, {}), {4}... | custom-call | flops 1207959552 | bytes 12582912 | tf_op jit(solution)/shard_map/fwd_half/pallas_call | solution.py:266
  150.4 7.8 %fwd_half.31 = (bf16[6,128,1536]{2,1,0:T(8,128)(2,1)S(1)}, bf16[6,128,1536]{2,1,0:T(8,128)(2,1)S(1)}, bf16[6,128,2304]{2,1,0:T(8,128)(2,1)S(1)}, bf16[6,128,768]...) custom-call(s32[1]{0:T(128)} %bitcast.sec, ...), custom_call_target="tpu_custom_call", output_to_operand_aliasing={{0}: (6, {}), {1}: (7, {}), {2}: (8, {}), {3}: (9, {}), {4}... | custom-call | flops 1207959552 | bytes 12582912 | tf_op jit(solution)/shard_map/fwd_half/pallas_call | solution.py:266
  159.0 44.8 %collective-permute-start.11 = (bf16[128,1536]{1,0:T(8,128)(2,1)S(1)}, bf16[128,1536]{1,0:T(8,128)(2,1)S(1)}, u32[]{:S(2)}, u32[]{:S(2)}) collective-permute-start(bf16[128,1536]{1,0:T(8,128)(2,1)S(1)} %get-tuple-element.387), channel_id=1, source_target_pairs={{64,80},{80,96},{96,112},{65,81},{81,97},{97,113},{66,82},{82,98},... | collective-permute-start | bytes 1179656 | tf_op jit(solution)/shard_map/ppermute | solution.py:365
  203.9 16.6 %collective-permute-start.14 = (bf16[128,1536]{1,0:T(8,128)(2,1)S(1)}, bf16[128,1536]{1,0:T(8,128)(2,1)S(1)}, u32[]{:S(2)}, u32[]{:S(2)}) collective-permute-start(bf16[128,1536]{1,0:T(8,128)(2,1)S(1)} %get-tuple-element.400), channel_id=1, source_target_pairs={{64,80},{80,96},{96,112},{65,81},{81,97},{97,113},{66,82},{82,98},... | collective-permute-start | bytes 1179656 | tf_op jit(solution)/shard_map/ppermute | solution.py:365
  222.9 6.7 fwd_half.35
  232.7 8.2 %bwd_half.21 = (bf16[6,128,1536]{2,1,0:T(8,128)(2,1)S(1)}, bf16[6,128,1536]{2,1,0:T(8,128)(2,1)S(1)}, bf16[6,128,2304]{2,1,0:T(8,128)(2,1)S(1)}, bf16[6,128,768]...) custom-call(s32[1]{0:T(128)} %bitcast.sec, ...), custom_call_target="tpu_custom_call", output_to_operand_aliasing={{0}: (6, {}), {1}: (7, {}), {2}: (8, {}), {3}: (9, {}), {4}... | custom-call | flops 2415919104 | bytes 12582912 | tf_op jit(solution)/shard_map/bwd_half/pallas_call | solution.py:266
  243.5 9.1 %bwd_half.23 = (bf16[6,128,1536]{2,1,0:T(8,128)(2,1)S(1)}, bf16[6,128,1536]{2,1,0:T(8,128)(2,1)S(1)}, bf16[6,128,2304]{2,1,0:T(8,128)(2,1)S(1)}, bf16[6,128,768]...) custom-call(s32[1]{0:T(128)} %bitcast.sec, ...), custom_call_target="tpu_custom_call", output_to_operand_aliasing={{0}: (6, {}), {1}: (7, {}), {2}: (8, {}), {3}: (9, {}), {4}... | custom-call | flops 2415919104 | bytes 12582912 | tf_op jit(solution)/shard_map/bwd_half/pallas_call | solution.py:266
  253.7 77.0 %collective-permute-start.23 = (bf16[128,1536]{1,0:T(8,128)(2,1)S(1)}, bf16[128,1536]{1,0:T(8,128)(2,1)S(1)}, u32[]{:S(2)}, u32[]{:S(2)}) collective-permute-start(bf16[128,1536]{1,0:T(8,128)(2,1)S(1)} %get-tuple-element.484), channel_id=1, source_target_pairs={{80,64},{96,80},{112,96},{81,65},{97,81},{113,97},{82,66},{98,82},... | collective-permute-start | bytes 1179656 | tf_op jit(solution)/shard_map/ppermute | solution.py:376
  331.0 18.9 %collective-permute-start.22 = (bf16[128,1536]{1,0:T(8,128)(2,1)S(1)}, bf16[128,1536]{1,0:T(8,128)(2,1)S(1)}, u32[]{:S(2)}, u32[]{:S(2)}) collective-permute-start(bf16[128,1536]{1,0:T(8,128)(2,1)S(1)} %get-tuple-element.483), channel_id=1, source_target_pairs={{80,64},{96,80},{112,96},{81,65},{97,81},{113,97},{82,66},{98,82},... | collective-permute-start | bytes 1179656 | tf_op jit(solution)/shard_map/ppermute | solution.py:376
  349.9 7.0 bwd_half.26
  356.9 12.9 %collective-permute-start.25 = (bf16[128,1536]{1,0:T(8,128)(2,1)S(1)}, bf16[128,1536]{1,0:T(8,128)(2,1)S(1)}, u32[]{:S(2)}, u32[]{:S(2)}) collective-permute-start(bf16[128,1536]{1,0:T(8,128)(2,1)S(1)} %get-tuple-element.504), channel_id=1, source_target_pairs={{64,48},{80,64},{96,80},{65,49},{81,65},{97,81},{66,50},{82,66},{9... | collective-permute-start | bytes 1179656 | tf_op jit(solution)/shard_map/ppermute | solution.py:376
  371.7 6.7 bwd_half.29
  380.9 7.8 %bwd_half.32 = (bf16[6,128,1536]{2,1,0:T(8,128)(2,1)S(1)}, bf16[6,128,1536]{2,1,0:T(8,128)(2,1)S(1)}, bf16[6,128,2304]{2,1,0:T(8,128)(2,1)S(1)}, bf16[6,128,768]...) custom-call(s32[1]{0:T(128)} %bitcast.sec, ...), custom_call_target="tpu_custom_call", output_to_operand_aliasing={{0}: (6, {}), {1}: (7, {}), {2}: (8, {}), {3}: (9, {}), {4}... | custom-call | flops 2415919104 | bytes 12582912 | tf_op jit(solution)/shard_map/bwd_half/pallas_call | solution.py:266
  388.7 1.3 collective-permute-start.31
  390.2 1.3 collective-permute-start.30
  391.5 54.0 %collective-permute-done.31.recv = bf16[128,1536]{1,0:T(8,128)(2,1)S(1)} collective-permute-done((bf16[128,1536]{1,0:T(8,128)(2,1)S(1)}, bf16[128,1536]{1,0:T(8,128)(2,1)S(1)}, u32[]{:S(2)}, u32[]{:S(2)}) %collective-permute-start.31) | collective-permute-done | bytes 393248 | tf_op jit(solution)/shard_map/ppermute | solution.py:376
  445.5 9.0 %bwd_half.34 = (bf16[6,128,1536]{2,1,0:T(8,128)(2,1)S(1)}, bf16[6,128,1536]{2,1,0:T(8,128)(2,1)S(1)}, bf16[6,128,2304]{2,1,0:T(8,128)(2,1)S(1)}, bf16[6,128,768]...) custom-call(s32[1]{0:T(128)} %bitcast.sec, ...), custom_call_target="tpu_custom_call", output_to_operand_aliasing={{0}: (6, {}), {1}: (7, {}), {2}: (8, {}), {3}: (9, {}), {4}... | custom-call | flops 2415919104 | bytes 12582912 | tf_op jit(solution)/shard_map/bwd_half/pallas_call | solution.py:266
  456.4 9.3 %bwd_half.35 = (bf16[6,128,1536]{2,1,0:T(8,128)(2,1)S(1)}, bf16[6,128,1536]{2,1,0:T(8,128)(2,1)S(1)}, bf16[6,128,2304]{2,1,0:T(8,128)(2,1)S(1)}, bf16[6,128,768]...) custom-call(s32[1]{0:T(128)} %bitcast.sec, ...), custom_call_target="tpu_custom_call", output_to_operand_aliasing={{0}: (6, {}), {1}: (7, {}), {2}: (8, {}), {3}: (9, {}), {4}... | custom-call | flops 2415919104 | bytes 12582912 | tf_op jit(solution)/shard_map/bwd_half/pallas_call | solution.py:266
  467.9 9.0 %bwd_half.36 = (bf16[6,128,1536]{2,1,0:T(8,128)(2,1)S(1)}, bf16[6,128,1536]{2,1,0:T(8,128)(2,1)S(1)}, bf16[6,128,2304]{2,1,0:T(8,128)(2,1)S(1)}, bf16[6,128,768]...) custom-call(s32[1]{0:T(128)} %bitcast.sec, ...), custom_call_target="tpu_custom_call", output_to_operand_aliasing={{0}: (6, {}), {1}: (7, {}), {2}: (8, {}), {3}: (9, {}), {4}... | custom-call | flops 2415919104 | bytes 12582912 | tf_op jit(solution)/shard_map/bwd_half/pallas_call | solution.py:266
  476.9 1.3 collective-permute-start.35
  479.1 8.9 %bwd_half.37 = (bf16[6,128,1536]{2,1,0:T(8,128)(2,1)S(1)}, bf16[6,128,1536]{2,1,0:T(8,128)(2,1)S(1)}, bf16[6,128,2304]{2,1,0:T(8,128)(2,1)S(1)}, bf16[6,128,768]...) custom-call(s32[1]{0:T(128)} %bitcast.sec, ...), custom_call_target="tpu_custom_call", output_to_operand_aliasing={{0}: (6, {}), {1}: (7, {}), {2}: (8, {}), {3}: (9, {}), {4}... | custom-call | flops 2415919104 | bytes 12582912 | tf_op jit(solution)/shard_map/bwd_half/pallas_call | solution.py:266
  489.5 10.1 %bwd_half.38 = (bf16[6,128,1536]{2,1,0:T(8,128)(2,1)S(1)}, bf16[6,128,1536]{2,1,0:T(8,128)(2,1)S(1)}, bf16[6,128,2304]{2,1,0:T(8,128)(2,1)S(1)}, bf16[6,128,768]...) custom-call(s32[1]{0:T(128)} %bitcast.sec, ...), custom_call_target="tpu_custom_call", output_to_operand_aliasing={{0}: (6, {}), {1}: (7, {}), {2}: (8, {}), {3}: (9, {}), {4}... | custom-call | flops 2415919104 | bytes 12582912 | tf_op jit(solution)/shard_map/bwd_half/pallas_call | solution.py:266
  499.8 9.5 %bwd_half.39 = (bf16[6,128,1536]{2,1,0:T(8,128)(2,1)S(1)}, bf16[6,128,1536]{2,1,0:T(8,128)(2,1)S(1)}, bf16[6,128,2304]{2,1,0:T(8,128)(2,1)S(1)}, bf16[6,128,768]...) custom-call(s32[1]{0:T(128)} %bitcast.sec, ...), custom_call_target="tpu_custom_call", output_to_operand_aliasing={{0}: (6, {}), {1}: (7, {}), {2}: (8, {}), {3}: (9, {}), {4}... | custom-call | flops 2415919104 | bytes 12582912 | tf_op jit(solution)/shard_map/bwd_half/pallas_call | solution.py:266
  509.3 1.8 copy-done.1
  511.0 3.5 bitcast_convert_fusion.1
  514.6 9.8 %bitcast_convert_fusion = bf16[1536,2304]{1,0:T(8,128)(2,1)} fusion(bf16[6,128,1536]{2,1,0:T(8,128)(2,1)S(1)} %get-tuple-element.623, bf16[6,128,2304]{2,1,0:T(8,128)(2,1)} %copy-done.1), kind=kOutput, calls=%fused_computation | convolution fusion | flops 5439356928 | bytes 12976128 | tf_op jit(solution)/shard_map/dot_general | solution.py:20
  525.7 2.1 collective-permute-start.38
  527.8 2.6 collective-permute-start.37
  532.7 3.0 collective-permute-done.40
  536.9 34.1 %reduce-scatter.5.cloned.1.call-done = bf16[48,1536]{1,0:T(8,128)(2,1)} async-done(((bf16[768,1536]{1,0:T(8,128)(2,1)}), bf16[48,1536]{1,0:T(8,128)(2,1)}) %reduce-scatter.5.cloned.1.call-update) | async-done | bytes 147472 | tf_op jit(solution)/shard_map/reduce_scatter | solution.py:382
  571.0 1.6 fusion.3
  572.6 71.0 %reduce-scatter.3.cloned.1.call-done = bf16[96,2304]{1,0:T(8,128)(2,1)} async-done(((bf16[1536,2304]{1,0:T(8,128)(2,1)}), bf16[96,2304]{1,0:T(8,128)(2,1)}) %reduce-scatter.3.cloned.1.call-update) | async-done | bytes 442384 | tf_op jit(solution)/shard_map/reduce_scatter | solution.py:383
  643.6 1.8 fusion
  648.6 4.2 collective-permute-start.43
  652.8 2.2 collective-permute-start.44
  655.0 1.6 collective-permute-done.44
  656.6 2.0 collective-permute-done.42
  658.6 6.7 collective-permute-start.47
  665.3 8.9 %collective-permute-start.46 = (f32[8,128]{1,0:T(8,128)S(1)}, f32[8,128]{1,0:T(8,128)S(1)}, u32[]{:S(2)}, u32[]{:S(2)}) collective-permute-start(f32[8,128]{1,0:T(8,128)S(1)} %add_add_fusion.3), channel_id=1, source_target_pairs={{0,64},{1,65},{2,66},{3,67},{4,68},{5,69},{6,70},{7,71},{8,72},{9,... | collective-permute-start | bytes 12296 | tf_op jit(solution)/shard_map/ppermute | solution.py:286
  674.2 1.5 collective-permute-start.45
  675.7 1.6 convert_bitcast_fusion.1
  677.3 1.4 collective-permute-done.46
  678.8 7.9 %collective-permute-start.50 = (f32[8,128]{1,0:T(8,128)S(1)}, f32[8,128]{1,0:T(8,128)S(1)}, u32[]{:S(2)}, u32[]{:S(2)}) collective-permute-start(f32[8,128]{1,0:T(8,128)S(1)} %add_add_fusion.2), channel_id=1, source_target_pairs={{0,48},{1,49},{2,50},{3,51},{4,52},{5,53},{6,54},{7,55},{8,56},{9,... | collective-permute-start | bytes 12296 | tf_op jit(solution)/shard_map/ppermute | solution.py:286
  686.7 8.9 %collective-permute-start.49 = (f32[8,128]{1,0:T(8,128)S(1)}, f32[8,128]{1,0:T(8,128)S(1)}, u32[]{:S(2)}, u32[]{:S(2)}) collective-permute-start(f32[8,128]{1,0:T(8,128)S(1)} %add_add_fusion.2), channel_id=1, source_target_pairs={{0,32},{1,33},{2,34},{3,35},{4,36},{5,37},{6,38},{7,39},{8,40},{9,... | collective-permute-start | bytes 12296 | tf_op jit(solution)/shard_map/ppermute | solution.py:286
  695.6 8.9 %collective-permute-start.48 = (f32[8,128]{1,0:T(8,128)S(1)}, f32[8,128]{1,0:T(8,128)S(1)}, u32[]{:S(2)}, u32[]{:S(2)}) collective-permute-start(f32[8,128]{1,0:T(8,128)S(1)} %add_add_fusion.2), channel_id=1, source_target_pairs={{0,16},{1,17},{2,18},{3,19},{4,20},{5,21},{6,22},{7,23},{8,24},{9,... | collective-permute-start | bytes 12296 | tf_op jit(solution)/shard_map/ppermute | solution.py:286
  704.5 2.0 convert_bitcast_fusion
  (136 shorter events, 36.6 us)
Async XLA Ops:
  7.2 4.7 copy-start.6
  7.2 62.4 %all-gather.3.cloned.1.call-start = ((), (), s32[]{:S(2)}) async-start(), calls=%async_computation.4 | async-start | bytes 10027008 | tf_op jit(solution)/shard_map/all_gather | solution.py:306
  10.1 560.9 %reduce-scatter.5.cloned.1.call-start = ((), (), s32[]{:S(2)}) async-start(), calls=%async_computation.3 | async-start | bytes 2506752 | tf_op jit(solution)/shard_map/reduce_scatter | solution.py:382
  69.6 0.8 copy-start.4
  69.6 3.7 copy-start
  73.3 1.7 copy-start.2
  81.9 10.7 %collective-permute-start = (bf16[128,1536]{1,0:T(8,128)(2,1)S(1)}, bf16[128,1536]{1,0:T(8,128)(2,1)S(1)}, u32[]{:S(2)}, u32[]{:S(2)}) collective-permute-start(bf16[128,1536]{1,0:T(8,128)(2,1)S(1)} %get-tuple-element.316), channel_id=1, source_target_pairs={{0,16},{1,17},{2,18},{3,19},{4,20},{5,21},{6,22},{7,23},{8,24},{9,... | collective-permute-start | bytes 1179656 | tf_op jit(solution)/shard_map/ppermute | solution.py:365
  89.8 14.2 %collective-permute-start.2 = (bf16[128,1536]{1,0:T(8,128)(2,1)S(1)}, bf16[128,1536]{1,0:T(8,128)(2,1)S(1)}, u32[]{:S(2)}, u32[]{:S(2)}) collective-permute-start(bf16[128,1536]{1,0:T(8,128)(2,1)S(1)} %get-tuple-element.328), channel_id=1, source_target_pairs={{0,16},{1,17},{2,18},{3,19},{4,20},{5,21},{6,22},{7,23},{8,24},{9,... | collective-permute-start | bytes 1179656 | tf_op jit(solution)/shard_map/ppermute | solution.py:365
  99.6 14.2 %collective-permute-start.1 = (bf16[128,1536]{1,0:T(8,128)(2,1)S(1)}, bf16[128,1536]{1,0:T(8,128)(2,1)S(1)}, u32[]{:S(2)}, u32[]{:S(2)}) collective-permute-start(bf16[128,1536]{1,0:T(8,128)(2,1)S(1)} %get-tuple-element.327), channel_id=1, source_target_pairs={{0,16},{16,32},{1,17},{17,33},{2,18},{18,34},{3,19},{19,35},{4,20}... | collective-permute-start | bytes 1179656 | tf_op jit(solution)/shard_map/ppermute | solution.py:365
  111.8 11.4 %collective-permute-start.4 = (bf16[128,1536]{1,0:T(8,128)(2,1)S(1)}, bf16[128,1536]{1,0:T(8,128)(2,1)S(1)}, u32[]{:S(2)}, u32[]{:S(2)}) collective-permute-start(bf16[128,1536]{1,0:T(8,128)(2,1)S(1)} %get-tuple-element.340), channel_id=1, source_target_pairs={{0,16},{16,32},{1,17},{17,33},{2,18},{18,34},{3,19},{19,35},{4,20}... | collective-permute-start | bytes 1179656 | tf_op jit(solution)/shard_map/ppermute | solution.py:365
  120.8 11.8 %collective-permute-start.3 = (bf16[128,1536]{1,0:T(8,128)(2,1)S(1)}, bf16[128,1536]{1,0:T(8,128)(2,1)S(1)}, u32[]{:S(2)}, u32[]{:S(2)}) collective-permute-start(bf16[128,1536]{1,0:T(8,128)(2,1)S(1)} %get-tuple-element.339), channel_id=1, source_target_pairs={{0,16},{16,32},{32,48},{1,17},{17,33},{33,49},{2,18},{18,34},{34,5... | collective-permute-start | bytes 1179656 | tf_op jit(solution)/shard_map/ppermute | solution.py:365
  129.8 9.7 %collective-permute-start.6 = (bf16[128,1536]{1,0:T(8,128)(2,1)S(1)}, bf16[128,1536]{1,0:T(8,128)(2,1)S(1)}, u32[]{:S(2)}, u32[]{:S(2)}) collective-permute-start(bf16[128,1536]{1,0:T(8,128)(2,1)S(1)} %get-tuple-element.352), channel_id=1, source_target_pairs={{0,16},{16,32},{32,48},{1,17},{17,33},{33,49},{2,18},{18,34},{34,5... | collective-permute-start | bytes 1179656 | tf_op jit(solution)/shard_map/ppermute | solution.py:365
  132.7 15.1 %collective-permute-start.5 = (bf16[128,1536]{1,0:T(8,128)(2,1)S(1)}, bf16[128,1536]{1,0:T(8,128)(2,1)S(1)}, u32[]{:S(2)}, u32[]{:S(2)}) collective-permute-start(bf16[128,1536]{1,0:T(8,128)(2,1)S(1)} %get-tuple-element.351), channel_id=1, source_target_pairs={{16,32},{32,48},{48,64},{17,33},{33,49},{49,65},{18,34},{34,50},{5... | collective-permute-start | bytes 1179656 | tf_op jit(solution)/shard_map/ppermute | solution.py:365
  147.1 1.6 collective-permute-start.8
  148.0 1.6 collective-permute-start.7
  148.8 1.6 collective-permute-start.10
  149.7 9.2 %collective-permute-start.9 = (bf16[128,1536]{1,0:T(8,128)(2,1)S(1)}, bf16[128,1536]{1,0:T(8,128)(2,1)S(1)}, u32[]{:S(2)}, u32[]{:S(2)}) collective-permute-start(bf16[128,1536]{1,0:T(8,128)(2,1)S(1)} %get-tuple-element.375), channel_id=1, source_target_pairs={{48,64},{64,80},{80,96},{49,65},{65,81},{81,97},{50,66},{66,82},{8... | collective-permute-start | bytes 1179656 | tf_op jit(solution)/shard_map/ppermute | solution.py:365
  158.2 45.6 %collective-permute-start.12 = (bf16[128,1536]{1,0:T(8,128)(2,1)S(1)}, bf16[128,1536]{1,0:T(8,128)(2,1)S(1)}, u32[]{:S(2)}, u32[]{:S(2)}) collective-permute-start(bf16[128,1536]{1,0:T(8,128)(2,1)S(1)} %get-tuple-element.388), channel_id=1, source_target_pairs={{48,64},{64,80},{80,96},{49,65},{65,81},{81,97},{50,66},{66,82},{8... | collective-permute-start | bytes 1179656 | tf_op jit(solution)/shard_map/ppermute | solution.py:365
  159.0 61.5 %collective-permute-start.11 = (bf16[128,1536]{1,0:T(8,128)(2,1)S(1)}, bf16[128,1536]{1,0:T(8,128)(2,1)S(1)}, u32[]{:S(2)}, u32[]{:S(2)}) collective-permute-start(bf16[128,1536]{1,0:T(8,128)(2,1)S(1)} %get-tuple-element.387), channel_id=1, source_target_pairs={{64,80},{80,96},{96,112},{65,81},{81,97},{97,113},{66,82},{82,98},... | collective-permute-start | bytes 1179656 | tf_op jit(solution)/shard_map/ppermute | solution.py:365
  203.9 18.8 %collective-permute-start.14 = (bf16[128,1536]{1,0:T(8,128)(2,1)S(1)}, bf16[128,1536]{1,0:T(8,128)(2,1)S(1)}, u32[]{:S(2)}, u32[]{:S(2)}) collective-permute-start(bf16[128,1536]{1,0:T(8,128)(2,1)S(1)} %get-tuple-element.400), channel_id=1, source_target_pairs={{64,80},{80,96},{96,112},{65,81},{81,97},{97,113},{66,82},{82,98},... | collective-permute-start | bytes 1179656 | tf_op jit(solution)/shard_map/ppermute | solution.py:365
  220.5 1.7 copy-start.5
  220.7 2.3 copy-start.3
  220.7 11.1 %collective-permute-start.13 = (bf16[128,1536]{1,0:T(8,128)(2,1)S(1)}, bf16[128,1536]{1,0:T(8,128)(2,1)S(1)}, u32[]{:S(2)}, u32[]{:S(2)}) collective-permute-start(bf16[128,1536]{1,0:T(8,128)(2,1)S(1)} %get-tuple-element.399), channel_id=1, source_target_pairs={{80,96},{96,112},{81,97},{97,113},{82,98},{98,114},{83,99},{99,115... | collective-permute-start | bytes 1179656 | tf_op jit(solution)/shard_map/ppermute | solution.py:365
  229.7 11.9 %collective-permute-start.18 = (bf16[128,1536]{1,0:T(8,128)(2,1)S(1)}, bf16[128,1536]{1,0:T(8,128)(2,1)S(1)}, u32[]{:S(2)}, u32[]{:S(2)}) collective-permute-start(bf16[128,1536]{1,0:T(8,128)(2,1)S(1)} %get-tuple-element.428), channel_id=1, source_target_pairs={{80,96},{96,112},{81,97},{97,113},{82,98},{98,114},{83,99},{99,115... | collective-permute-start | bytes 1179656 | tf_op jit(solution)/shard_map/ppermute | solution.py:365
  231.1 10.6 %collective-permute-start.17 = (bf16[128,1536]{1,0:T(8,128)(2,1)S(1)}, bf16[128,1536]{1,0:T(8,128)(2,1)S(1)}, u32[]{:S(2)}, u32[]{:S(2)}) collective-permute-start(bf16[128,1536]{1,0:T(8,128)(2,1)S(1)} %get-tuple-element.427), channel_id=1, source_target_pairs={{112,96},{113,97},{114,98},{115,99},{116,100},{117,101},{118,102},... | collective-permute-start | bytes 1179656 | tf_op jit(solution)/shard_map/ppermute | solution.py:376
  232.0 11.4 %collective-permute-start.16 = (bf16[128,1536]{1,0:T(8,128)(2,1)S(1)}, bf16[128,1536]{1,0:T(8,128)(2,1)S(1)}, u32[]{:S(2)}, u32[]{:S(2)}) collective-permute-start(bf16[128,1536]{1,0:T(8,128)(2,1)S(1)} %get-tuple-element.426), channel_id=1, source_target_pairs={{96,112},{97,113},{98,114},{99,115},{100,116},{101,117},{102,118},... | collective-permute-start | bytes 1179656 | tf_op jit(solution)/shard_map/ppermute | solution.py:365
  240.9 2.6 collective-permute-start.15
  242.0 11.5 %collective-permute-start.20 = (bf16[128,1536]{1,0:T(8,128)(2,1)S(1)}, bf16[128,1536]{1,0:T(8,128)(2,1)S(1)}, u32[]{:S(2)}, u32[]{:S(2)}) collective-permute-start(bf16[128,1536]{1,0:T(8,128)(2,1)S(1)} %get-tuple-element.458), channel_id=1, source_target_pairs={{96,80},{112,96},{97,81},{113,97},{98,82},{114,98},{99,83},{115,99... | collective-permute-start | bytes 1179656 | tf_op jit(solution)/shard_map/ppermute | solution.py:376
  242.6 10.7 %collective-permute-start.21 = (bf16[128,1536]{1,0:T(8,128)(2,1)S(1)}, bf16[128,1536]{1,0:T(8,128)(2,1)S(1)}, u32[]{:S(2)}, u32[]{:S(2)}) collective-permute-start(bf16[128,1536]{1,0:T(8,128)(2,1)S(1)} %get-tuple-element.459), channel_id=1, source_target_pairs={{96,112},{97,113},{98,114},{99,115},{100,116},{101,117},{102,118},... | collective-permute-start | bytes 1179656 | tf_op jit(solution)/shard_map/ppermute | solution.py:365
  252.6 78.1 %collective-permute-start.19 = (bf16[128,1536]{1,0:T(8,128)(2,1)S(1)}, bf16[128,1536]{1,0:T(8,128)(2,1)S(1)}, u32[]{:S(2)}, u32[]{:S(2)}) collective-permute-start(bf16[128,1536]{1,0:T(8,128)(2,1)S(1)} %get-tuple-element.457), channel_id=1, source_target_pairs={{96,80},{112,96},{97,81},{113,97},{98,82},{114,98},{99,83},{115,99... | collective-permute-start | bytes 1179656 | tf_op jit(solution)/shard_map/ppermute | solution.py:376
  253.7 96.2 %collective-permute-start.23 = (bf16[128,1536]{1,0:T(8,128)(2,1)S(1)}, bf16[128,1536]{1,0:T(8,128)(2,1)S(1)}, u32[]{:S(2)}, u32[]{:S(2)}) collective-permute-start(bf16[128,1536]{1,0:T(8,128)(2,1)S(1)} %get-tuple-element.484), channel_id=1, source_target_pairs={{80,64},{96,80},{112,96},{81,65},{97,81},{113,97},{82,66},{98,82},... | collective-permute-start | bytes 1179656 | tf_op jit(solution)/shard_map/ppermute | solution.py:376
  331.0 38.9 %collective-permute-start.22 = (bf16[128,1536]{1,0:T(8,128)(2,1)S(1)}, bf16[128,1536]{1,0:T(8,128)(2,1)S(1)}, u32[]{:S(2)}, u32[]{:S(2)}) collective-permute-start(bf16[128,1536]{1,0:T(8,128)(2,1)S(1)} %get-tuple-element.483), channel_id=1, source_target_pairs={{80,64},{96,80},{112,96},{81,65},{97,81},{113,97},{82,66},{98,82},... | collective-permute-start | bytes 1179656 | tf_op jit(solution)/shard_map/ppermute | solution.py:376
  356.9 13.9 %collective-permute-start.25 = (bf16[128,1536]{1,0:T(8,128)(2,1)S(1)}, bf16[128,1536]{1,0:T(8,128)(2,1)S(1)}, u32[]{:S(2)}, u32[]{:S(2)}) collective-permute-start(bf16[128,1536]{1,0:T(8,128)(2,1)S(1)} %get-tuple-element.504), channel_id=1, source_target_pairs={{64,48},{80,64},{96,80},{65,49},{81,65},{97,81},{66,50},{82,66},{9... | collective-permute-start | bytes 1179656 | tf_op jit(solution)/shard_map/ppermute | solution.py:376
  370.1 1.6 collective-permute-start.24
  371.0 8.2 %collective-permute-start.27 = (bf16[128,1536]{1,0:T(8,128)(2,1)S(1)}, bf16[128,1536]{1,0:T(8,128)(2,1)S(1)}, u32[]{:S(2)}, u32[]{:S(2)}) collective-permute-start(bf16[128,1536]{1,0:T(8,128)(2,1)S(1)} %get-tuple-element.524), channel_id=1, source_target_pairs={{48,32},{64,48},{80,64},{49,33},{65,49},{81,65},{50,34},{66,50},{8... | collective-permute-start | bytes 1179656 | tf_op jit(solution)/shard_map/ppermute | solution.py:376
  378.4 1.6 collective-permute-start.26
  379.3 1.6 collective-permute-start.29
  380.2 9.8 %collective-permute-start.28 = (bf16[128,1536]{1,0:T(8,128)(2,1)S(1)}, bf16[128,1536]{1,0:T(8,128)(2,1)S(1)}, u32[]{:S(2)}, u32[]{:S(2)}) collective-permute-start(bf16[128,1536]{1,0:T(8,128)(2,1)S(1)} %get-tuple-element.543), channel_id=1, source_target_pairs={{32,16},{48,32},{64,48},{33,17},{49,33},{65,49},{34,18},{50,34},{6... | collective-permute-start | bytes 1179656 | tf_op jit(solution)/shard_map/ppermute | solution.py:376
  388.7 56.8 %collective-permute-start.31 = (bf16[128,1536]{1,0:T(8,128)(2,1)S(1)}, bf16[128,1536]{1,0:T(8,128)(2,1)S(1)}, u32[]{:S(2)}, u32[]{:S(2)}) collective-permute-start(bf16[128,1536]{1,0:T(8,128)(2,1)S(1)} %get-tuple-element.564), channel_id=1, source_target_pairs={{16,0},{32,16},{48,32},{17,1},{33,17},{49,33},{18,2},{34,18},{50,3... | collective-permute-start | bytes 1179656 | tf_op jit(solution)/shard_map/ppermute | solution.py:376
  390.2 66.2 %collective-permute-start.30 = (bf16[128,1536]{1,0:T(8,128)(2,1)S(1)}, bf16[128,1536]{1,0:T(8,128)(2,1)S(1)}, u32[]{:S(2)}, u32[]{:S(2)}) collective-permute-start(bf16[128,1536]{1,0:T(8,128)(2,1)S(1)} %get-tuple-element.563), channel_id=1, source_target_pairs={{16,0},{32,16},{48,32},{17,1},{33,17},{49,33},{18,2},{34,18},{50,3... | collective-permute-start | bytes 1179656 | tf_op jit(solution)/shard_map/ppermute | solution.py:376
  454.5 13.3 %collective-permute-start.33 = (bf16[128,1536]{1,0:T(8,128)(2,1)S(1)}, bf16[128,1536]{1,0:T(8,128)(2,1)S(1)}, u32[]{:S(2)}, u32[]{:S(2)}) collective-permute-start(bf16[128,1536]{1,0:T(8,128)(2,1)S(1)} %get-tuple-element.584), channel_id=1, source_target_pairs={{16,0},{32,16},{17,1},{33,17},{18,2},{34,18},{19,3},{35,19},{20,4}... | collective-permute-start | bytes 1179656 | tf_op jit(solution)/shard_map/ppermute | solution.py:376
  465.7 13.5 %collective-permute-start.32 = (bf16[128,1536]{1,0:T(8,128)(2,1)S(1)}, bf16[128,1536]{1,0:T(8,128)(2,1)S(1)}, u32[]{:S(2)}, u32[]{:S(2)}) collective-permute-start(bf16[128,1536]{1,0:T(8,128)(2,1)S(1)} %get-tuple-element.583), channel_id=1, source_target_pairs={{16,0},{32,16},{17,1},{33,17},{18,2},{34,18},{19,3},{35,19},{20,4}... | collective-permute-start | bytes 1179656 | tf_op jit(solution)/shard_map/ppermute | solution.py:376
  476.9 12.6 %collective-permute-start.35 = (bf16[128,1536]{1,0:T(8,128)(2,1)S(1)}, bf16[128,1536]{1,0:T(8,128)(2,1)S(1)}, u32[]{:S(2)}, u32[]{:S(2)}) collective-permute-start(bf16[128,1536]{1,0:T(8,128)(2,1)S(1)} %get-tuple-element.604), channel_id=1, source_target_pairs={{16,0},{17,1},{18,2},{19,3},{20,4},{21,5},{22,6},{23,7},{24,8},{25... | collective-permute-start | bytes 1179656 | tf_op jit(solution)/shard_map/ppermute | solution.py:376
  488.0 11.7 %collective-permute-start.34 = (bf16[128,1536]{1,0:T(8,128)(2,1)S(1)}, bf16[128,1536]{1,0:T(8,128)(2,1)S(1)}, u32[]{:S(2)}, u32[]{:S(2)}) collective-permute-start(bf16[128,1536]{1,0:T(8,128)(2,1)S(1)} %get-tuple-element.603), channel_id=1, source_target_pairs={{16,0},{17,1},{18,2},{19,3},{20,4},{21,5},{22,6},{23,7},{24,8},{25... | collective-permute-start | bytes 1179656 | tf_op jit(solution)/shard_map/ppermute | solution.py:376
  509.3 1.8 copy-start.1
  514.6 129.0 %reduce-scatter.3.cloned.1.call-start = ((), (), s32[]{:S(2)}) async-start(), calls=%async_computation.2 | async-start | bytes 7520256 | tf_op jit(solution)/shard_map/reduce_scatter | solution.py:383
  524.5 1.3 collective-permute-start.36
  525.7 5.2 collective-permute-start.38
  527.8 3.7 collective-permute-start.39
  527.8 4.2 collective-permute-start.37
  532.1 3.7 collective-permute-start.40
  647.4 1.2 collective-permute-start.41
  648.6 6.4 collective-permute-start.43
  652.8 3.8 collective-permute-start.44
  655.0 3.6 collective-permute-start.42
  658.6 18.7 %collective-permute-start.47 = (f32[8,128]{1,0:T(8,128)S(1)}, f32[8,128]{1,0:T(8,128)S(1)}, u32[]{:S(2)}, u32[]{:S(2)}) collective-permute-start(f32[8,128]{1,0:T(8,128)S(1)} %add_add_fusion.3), channel_id=1, source_target_pairs={{0,72},{1,73},{2,74},{3,75},{4,76},{5,77},{6,78},{7,79},{8,64},{9,... | collective-permute-start | bytes 12296 | tf_op jit(solution)/shard_map/ppermute | solution.py:286
  665.3 13.5 %collective-permute-start.46 = (f32[8,128]{1,0:T(8,128)S(1)}, f32[8,128]{1,0:T(8,128)S(1)}, u32[]{:S(2)}, u32[]{:S(2)}) collective-permute-start(f32[8,128]{1,0:T(8,128)S(1)} %add_add_fusion.3), channel_id=1, source_target_pairs={{0,64},{1,65},{2,66},{3,67},{4,68},{5,69},{6,70},{7,71},{8,72},{9,... | collective-permute-start | bytes 12296 | tf_op jit(solution)/shard_map/ppermute | solution.py:286
  674.2 4.6 collective-permute-start.45
  678.8 27.7 %collective-permute-start.50 = (f32[8,128]{1,0:T(8,128)S(1)}, f32[8,128]{1,0:T(8,128)S(1)}, u32[]{:S(2)}, u32[]{:S(2)}) collective-permute-start(f32[8,128]{1,0:T(8,128)S(1)} %add_add_fusion.2), channel_id=1, source_target_pairs={{0,48},{1,49},{2,50},{3,51},{4,52},{5,53},{6,54},{7,55},{8,56},{9,... | collective-permute-start | bytes 12296 | tf_op jit(solution)/shard_map/ppermute | solution.py:286
  686.7 19.8 %collective-permute-start.49 = (f32[8,128]{1,0:T(8,128)S(1)}, f32[8,128]{1,0:T(8,128)S(1)}, u32[]{:S(2)}, u32[]{:S(2)}) collective-permute-start(f32[8,128]{1,0:T(8,128)S(1)} %add_add_fusion.2), channel_id=1, source_target_pairs={{0,32},{1,33},{2,34},{3,35},{4,36},{5,37},{6,38},{7,39},{8,40},{9,... | collective-permute-start | bytes 12296 | tf_op jit(solution)/shard_map/ppermute | solution.py:286
  695.6 12.1 %collective-permute-start.48 = (f32[8,128]{1,0:T(8,128)S(1)}, f32[8,128]{1,0:T(8,128)S(1)}, u32[]{:S(2)}, u32[]{:S(2)}) collective-permute-start(f32[8,128]{1,0:T(8,128)S(1)} %add_add_fusion.2), channel_id=1, source_target_pairs={{0,16},{1,17},{2,18},{3,19},{4,20},{5,21},{6,22},{7,23},{8,24},{9,... | collective-permute-start | bytes 12296 | tf_op jit(solution)/shard_map/ppermute | solution.py:286
Sparse Core Ops, SparseCore 0:
  10.3 59.2 all-gather.2
  514.7 56.2 reduce-scatter.4
  573.4 70.0 reduce-scatter.2

commit v2 on v1

--- a/solution.py
+++ b/solution.py
@@ -277,10 +277,18 @@
     return got[-1], list(got[:-1])
 
 
+def pair_set(on, low, high, size):
+    hops = [s for s in on if low <= s < high]
+    if not hops:
+        return []
+    start = min(max(hops[-1] - size + 1, low), high - size)
+    return list(range(start, start + size))
+
+
 def spread_sum(value, whole):
     rounds = [[1], [2, 4, 6], [8]]
     if whole:
-        rounds = [[1], [2, 4, 6], [8, 64, 72], [16, 32, 48]]
+        rounds = [[1], [2, 4, 6], [8], [64], [16, 32, 48]]
     for masks in rounds:
         got = [
             lax.ppermute(value, ("section", "dp"), [(i, i ^ mask) for i in range(128)])
@@ -360,8 +368,9 @@
                 [SMEM, ANY, ANY, ANY, VMEM, ANY],
                 states[:5], moved, f_scratch, ROWS * per_row, "fwd_half",
             )
-            pairs = [(s, s + 1) for s in on if s < last]
+            pairs = pair_set(on, 0, last, micro // 2)
             if pairs:
+                pairs = [(s, s + 1) for s in pairs]
                 f_recv[cycle + 2] = lax.ppermute(out, "section", pairs)
         on = [s for s in range(sections) if 0 <= cycle - first - 2 * (last - s) < micro]
         if on:
@@ -371,8 +380,9 @@
                 [SMEM, ANY, ANY, ANY, VMEM, ANY],
                 states, moved, b_scratch, 2 * ROWS * per_row, "bwd_half",
             )
-            pairs = [(s, s - 1) for s in on if s > 0]
+            pairs = pair_set([s - 1 for s in on], 0, last, micro // 2)
             if pairs:
+                pairs = [(s + 1, s) for s in pairs]
                 b_recv[cycle + 2] = lax.ppermute(out, "section", pairs)
     sa, so, sg, sd, sn = states[1], states[3], states[5], states[6], states[7]
     tokens = micro * ROWS

time: 726 us -> 644 us (0.89)
  starting transfers between devices: 260 us -> 59.7 us
  waiting for transfers between devices: 240 us -> 358 us
    ppermute x18, waiting for transfers between devices: 56.7 us -> 170 us  [local(): b_recv[cycle + 2] = lax.ppermute(out, 'section', pairs)]
    ppermute x18, starting transfers between devices: 123 us -> 16 us  [local(): b_recv[cycle + 2] = lax.ppermute(out, 'section', pairs)]
    ppermute x18, starting transfers between devices: 82.5 us -> 22.5 us  [local(): f_recv[cycle + 2] = lax.ppermute(out, 'section', pairs)]
    ppermute x15 -> x14, starting transfers between devices: 54.6 us -> 21 us  [spread_sum(): lax.ppermute(value, ('section', 'dp'), [(i, i ^ mask) for i in range(128)])]
    ppermute x15 -> x14, waiting for transfers between devices: 13.2 us -> 16.2 us  [spread_sum(): lax.ppermute(value, ('section', 'dp'), [(i, i ^ mask) for i in range(128)])]
  transfers between devices with their start and end apart: 54 -> 53, of which waited for: 21 -> 21; matrix products, arithmetic and copies ran while one was open for 3% -> 3% of each run, Pallas kernels for 20% -> 23%
where the time goes in v2:
time: 644 us; the launch traced here: 635 us
  waiting for transfers between devices  358 us (56%)
  Pallas kernels  163 us (25%)
  starting transfers between devices  59.7 us (9%)
  between operations  19.1 us (3%)
  matrix products  13.3 us (2%)
  local copies, waits for them, and re-layouts  11.7 us (2%)
  other arithmetic  10.9 us (2%)
    ppermute x18, waiting for transfers between devices, local(): b_recv[cycle + 2] = lax.ppermute(out, 'section', pairs)  170 us
    pallas_call x40, Pallas kernels, call(): pl.pallas_call(body, out_shape=shapes + [out_shape], in_specs=in_specs +...  163 us
    reduce_scatter x1, waiting for transfers between devices, local(): lax.psum_scatter(in_part, 'dp', scatter_dimension=0, tiled=True).astype(F32)  71.2 us
    all_gather x1, waiting for transfers between devices, local(): lax.all_gather(jnp.concatenate([in_proj[0], wo], axis=1), 'dp', axis=0)  57.5 us
    reduce_scatter x1, waiting for transfers between devices, local(): lax.psum_scatter(out_part, 'dp', scatter_dimension=0, tiled=True)  34.7 us
    ppermute x18, starting transfers between devices, local(): f_recv[cycle + 2] = lax.ppermute(out, 'section', pairs)  22.5 us
    ppermute x14, starting transfers between devices, spread_sum(): lax.ppermute(value, ('section', 'dp'), [(i, i ^ mask) for i in range(128)])  21 us
    ppermute x14, waiting for transfers between devices, spread_sum(): lax.ppermute(value, ('section', 'dp'), [(i, i ^ mask) for i in range(128)])  16.2 us
  transfers between devices with their start and end apart: 53, of which 21 were waited for; matrix products, arithmetic and copies ran while one was open for 3% of the time, Pallas kernels for 23%

profile of v2, /device:TPU:2, one launch (start us, length us, event | category | flops | bytes accessed | tf_op | source)
XLA Modules:
  0.0 634.9 jit_solution(12919721117069893223)
XLA Ops:
  8.2 1.9 maximum_maximum_fusion
  12.1 57.5 %all-gather.3.cloned.1.call-done = bf16[1536,3072]{1,0:T(8,128)(2,1)} async-done(((bf16[96,3072]{1,0:T(8,128)(2,1)}), bf16[1536,3072]{1,0:T(8,128)(2,1)}) %all-gather.3.cloned.1.call-update) | async-done | bytes 9437200 | tf_op jit(solution)/shard_map/all_gather | solution.py:314
  70.4 2.9 copy-done
  73.3 1.7 copy-done.2
  75.0 7.0 %fwd_half.20 = (bf16[6,128,1536]{2,1,0:T(8,128)(2,1)S(1)}, bf16[6,128,1536]{2,1,0:T(8,128)(2,1)S(1)}, bf16[6,128,2304]{2,1,0:T(8,128)(2,1)S(1)}, bf16[6,128,768]...) custom-call(s32[1]{0:T(128)} %bitcast.sec, ...), custom_call_target="tpu_custom_call", output_to_operand_aliasing={{0}: (6, {}), {1}: (7, {}), {2}: (8, {}), {3}: (9, {}), {4}... | custom-call | flops 1207959552 | bytes 12582912 | tf_op jit(solution)/shard_map/fwd_half/pallas_call | solution.py:266
  82.0 1.3 collective-permute-start
  83.3 6.5 %fwd_half.21 = (bf16[6,128,1536]{2,1,0:T(8,128)(2,1)S(1)}, bf16[6,128,1536]{2,1,0:T(8,128)(2,1)S(1)}, bf16[6,128,2304]{2,1,0:T(8,128)(2,1)S(1)}, bf16[6,128,768]...) custom-call(s32[1]{0:T(128)} %bitcast.sec, ...), custom_call_target="tpu_custom_call", output_to_operand_aliasing={{0}: (6, {}), {1}: (7, {}), {2}: (8, {}), {3}: (9, {}), {4}... | custom-call | flops 1207959552 | bytes 12582912 | tf_op jit(solution)/shard_map/fwd_half/pallas_call | solution.py:266
  89.8 1.3 collective-permute-start.2
  91.1 1.5 collective-permute-done.recv
  92.7 7.0 %fwd_half.22 = (bf16[6,128,1536]{2,1,0:T(8,128)(2,1)S(1)}, bf16[6,128,1536]{2,1,0:T(8,128)(2,1)S(1)}, bf16[6,128,2304]{2,1,0:T(8,128)(2,1)S(1)}, bf16[6,128,768]...) custom-call(s32[1]{0:T(128)} %bitcast.sec, ...), custom_call_target="tpu_custom_call", output_to_operand_aliasing={{0}: (6, {}), {1}: (7, {}), {2}: (8, {}), {3}: (9, {}), {4}... | custom-call | flops 1207959552 | bytes 12582912 | tf_op jit(solution)/shard_map/fwd_half/pallas_call | solution.py:266
  99.6 4.4 collective-permute-start.1
  104.0 7.8 %fwd_half.23 = (bf16[6,128,1536]{2,1,0:T(8,128)(2,1)S(1)}, bf16[6,128,1536]{2,1,0:T(8,128)(2,1)S(1)}, bf16[6,128,2304]{2,1,0:T(8,128)(2,1)S(1)}, bf16[6,128,768]...) custom-call(s32[1]{0:T(128)} %bitcast.sec, ...), custom_call_target="tpu_custom_call", output_to_operand_aliasing={{0}: (6, {}), {1}: (7, {}), {2}: (8, {}), {3}: (9, {}), {4}... | custom-call | flops 1207959552 | bytes 12582912 | tf_op jit(solution)/shard_map/fwd_half/pallas_call | solution.py:266
  111.9 1.9 collective-permute-start.4
  113.8 7.0 %fwd_half.24 = (bf16[6,128,1536]{2,1,0:T(8,128)(2,1)S(1)}, bf16[6,128,1536]{2,1,0:T(8,128)(2,1)S(1)}, bf16[6,128,2304]{2,1,0:T(8,128)(2,1)S(1)}, bf16[6,128,768]...) custom-call(s32[1]{0:T(128)} %bitcast.sec, ...), custom_call_target="tpu_custom_call", output_to_operand_aliasing={{0}: (6, {}), {1}: (7, {}), {2}: (8, {}), {3}: (9, {}), {4}... | custom-call | flops 1207959552 | bytes 12582912 | tf_op jit(solution)/shard_map/fwd_half/pallas_call | solution.py:266
  120.8 2.5 collective-permute-start.3
  123.3 6.5 %fwd_half.25 = (bf16[6,128,1536]{2,1,0:T(8,128)(2,1)S(1)}, bf16[6,128,1536]{2,1,0:T(8,128)(2,1)S(1)}, bf16[6,128,2304]{2,1,0:T(8,128)(2,1)S(1)}, bf16[6,128,768]...) custom-call(s32[1]{0:T(128)} %bitcast.sec, ...), custom_call_target="tpu_custom_call", output_to_operand_aliasing={{0}: (6, {}), {1}: (7, {}), {2}: (8, {}), {3}: (9, {}), {4}... | custom-call | flops 1207959552 | bytes 12582912 | tf_op jit(solution)/shard_map/fwd_half/pallas_call | solution.py:266
  129.8 2.7 collective-permute-start.6
  133.4 6.1 collective-permute-done.6.recv
  139.5 7.6 %fwd_half.27 = (bf16[6,128,1536]{2,1,0:T(8,128)(2,1)S(1)}, bf16[6,128,1536]{2,1,0:T(8,128)(2,1)S(1)}, bf16[6,128,2304]{2,1,0:T(8,128)(2,1)S(1)}, bf16[6,128,768]...) custom-call(s32[1]{0:T(128)} %bitcast.sec, ...), custom_call_target="tpu_custom_call", output_to_operand_aliasing={{0}: (6, {}), {1}: (7, {}), {2}: (8, {}), {3}: (9, {}), {4}... | custom-call | flops 1207959552 | bytes 12582912 | tf_op jit(solution)/shard_map/fwd_half/pallas_call | solution.py:266
  150.4 7.8 %fwd_half.31 = (bf16[6,128,1536]{2,1,0:T(8,128)(2,1)S(1)}, bf16[6,128,1536]{2,1,0:T(8,128)(2,1)S(1)}, bf16[6,128,2304]{2,1,0:T(8,128)(2,1)S(1)}, bf16[6,128,768]...) custom-call(s32[1]{0:T(128)} %bitcast.sec, ...), custom_call_target="tpu_custom_call", output_to_operand_aliasing={{0}: (6, {}), {1}: (7, {}), {2}: (8, {}), {3}: (9, {}), {4}... | custom-call | flops 1207959552 | bytes 12582912 | tf_op jit(solution)/shard_map/fwd_half/pallas_call | solution.py:266
  163.0 6.7 %fwd_half.35 = (bf16[6,128,1536]{2,1,0:T(8,128)(2,1)S(1)}, bf16[6,128,1536]{2,1,0:T(8,128)(2,1)S(1)}, bf16[6,128,2304]{2,1,0:T(8,128)(2,1)S(1)}, bf16[6,128,768]...) custom-call(s32[1]{0:T(128)} %bitcast.sec, ...), custom_call_target="tpu_custom_call", output_to_operand_aliasing={{0}: (6, {}), {1}: (7, {}), {2}: (8, {}), {3}: (9, {}), {4}... | custom-call | flops 1207959552 | bytes 12582912 | tf_op jit(solution)/shard_map/fwd_half/pallas_call | solution.py:266
  172.7 8.2 %bwd_half.21 = (bf16[6,128,1536]{2,1,0:T(8,128)(2,1)S(1)}, bf16[6,128,1536]{2,1,0:T(8,128)(2,1)S(1)}, bf16[6,128,2304]{2,1,0:T(8,128)(2,1)S(1)}, bf16[6,128,768]...) custom-call(s32[1]{0:T(128)} %bitcast.sec, ...), custom_call_target="tpu_custom_call", output_to_operand_aliasing={{0}: (6, {}), {1}: (7, {}), {2}: (8, {}), {3}: (9, {}), {4}... | custom-call | flops 2415919104 | bytes 12582912 | tf_op jit(solution)/shard_map/bwd_half/pallas_call | solution.py:266
  183.6 9.1 %bwd_half.23 = (bf16[6,128,1536]{2,1,0:T(8,128)(2,1)S(1)}, bf16[6,128,1536]{2,1,0:T(8,128)(2,1)S(1)}, bf16[6,128,2304]{2,1,0:T(8,128)(2,1)S(1)}, bf16[6,128,768]...) custom-call(s32[1]{0:T(128)} %bitcast.sec, ...), custom_call_target="tpu_custom_call", output_to_operand_aliasing={{0}: (6, {}), {1}: (7, {}), {2}: (8, {}), {3}: (9, {}), {4}... | custom-call | flops 2415919104 | bytes 12582912 | tf_op jit(solution)/shard_map/bwd_half/pallas_call | solution.py:266
  195.4 7.5 %bwd_half.26 = (bf16[6,128,1536]{2,1,0:T(8,128)(2,1)S(1)}, bf16[6,128,1536]{2,1,0:T(8,128)(2,1)S(1)}, bf16[6,128,2304]{2,1,0:T(8,128)(2,1)S(1)}, bf16[6,128,768]...) custom-call(s32[1]{0:T(128)} %bitcast.sec, ...), custom_call_target="tpu_custom_call", output_to_operand_aliasing={{0}: (6, {}), {1}: (7, {}), {2}: (8, {}), {3}: (9, {}), {4}... | custom-call | flops 2415919104 | bytes 12582912 | tf_op jit(solution)/shard_map/bwd_half/pallas_call | solution.py:266
  205.4 7.2 %bwd_half.29 = (bf16[6,128,1536]{2,1,0:T(8,128)(2,1)S(1)}, bf16[6,128,1536]{2,1,0:T(8,128)(2,1)S(1)}, bf16[6,128,2304]{2,1,0:T(8,128)(2,1)S(1)}, bf16[6,128,768]...) custom-call(s32[1]{0:T(128)} %bitcast.sec, ...), custom_call_target="tpu_custom_call", output_to_operand_aliasing={{0}: (6, {}), {1}: (7, {}), {2}: (8, {}), {3}: (9, {}), {4}... | custom-call | flops 2415919104 | bytes 12582912 | tf_op jit(solution)/shard_map/bwd_half/pallas_call | solution.py:266
  215.1 7.8 %bwd_half.32 = (bf16[6,128,1536]{2,1,0:T(8,128)(2,1)S(1)}, bf16[6,128,1536]{2,1,0:T(8,128)(2,1)S(1)}, bf16[6,128,2304]{2,1,0:T(8,128)(2,1)S(1)}, bf16[6,128,768]...) custom-call(s32[1]{0:T(128)} %bitcast.sec, ...), custom_call_target="tpu_custom_call", output_to_operand_aliasing={{0}: (6, {}), {1}: (7, {}), {2}: (8, {}), {3}: (9, {}), {4}... | custom-call | flops 2415919104 | bytes 12582912 | tf_op jit(solution)/shard_map/bwd_half/pallas_call | solution.py:266
  222.9 1.3 collective-permute-start.31
  224.4 1.3 collective-permute-start.30
  225.7 165.2 %collective-permute-done.31.recv = bf16[128,1536]{1,0:T(8,128)(2,1)S(1)} collective-permute-done((bf16[128,1536]{1,0:T(8,128)(2,1)S(1)}, bf16[128,1536]{1,0:T(8,128)(2,1)S(1)}, u32[]{:S(2)}, u32[]{:S(2)}) %collective-permute-start.31) | collective-permute-done | bytes 393248 | tf_op jit(solution)/shard_map/ppermute | solution.py:386
  390.8 9.0 %bwd_half.34 = (bf16[6,128,1536]{2,1,0:T(8,128)(2,1)S(1)}, bf16[6,128,1536]{2,1,0:T(8,128)(2,1)S(1)}, bf16[6,128,2304]{2,1,0:T(8,128)(2,1)S(1)}, bf16[6,128,768]...) custom-call(s32[1]{0:T(128)} %bitcast.sec, ...), custom_call_target="tpu_custom_call", output_to_operand_aliasing={{0}: (6, {}), {1}: (7, {}), {2}: (8, {}), {3}: (9, {}), {4}... | custom-call | flops 2415919104 | bytes 12582912 | tf_op jit(solution)/shard_map/bwd_half/pallas_call | solution.py:266
  399.9 1.3 collective-permute-start.33
  401.2 3.0 collective-permute-done.30.recv
  404.1 9.3 %bwd_half.35 = (bf16[6,128,1536]{2,1,0:T(8,128)(2,1)S(1)}, bf16[6,128,1536]{2,1,0:T(8,128)(2,1)S(1)}, bf16[6,128,2304]{2,1,0:T(8,128)(2,1)S(1)}, bf16[6,128,768]...) custom-call(s32[1]{0:T(128)} %bitcast.sec, ...), custom_call_target="tpu_custom_call", output_to_operand_aliasing={{0}: (6, {}), {1}: (7, {}), {2}: (8, {}), {3}: (9, {}), {4}... | custom-call | flops 2415919104 | bytes 12582912 | tf_op jit(solution)/shard_map/bwd_half/pallas_call | solution.py:266
  413.4 1.3 collective-permute-start.32
  415.4 9.0 %bwd_half.36 = (bf16[6,128,1536]{2,1,0:T(8,128)(2,1)S(1)}, bf16[6,128,1536]{2,1,0:T(8,128)(2,1)S(1)}, bf16[6,128,2304]{2,1,0:T(8,128)(2,1)S(1)}, bf16[6,128,768]...) custom-call(s32[1]{0:T(128)} %bitcast.sec, ...), custom_call_target="tpu_custom_call", output_to_operand_aliasing={{0}: (6, {}), {1}: (7, {}), {2}: (8, {}), {3}: (9, {}), {4}... | custom-call | flops 2415919104 | bytes 12582912 | tf_op jit(solution)/shard_map/bwd_half/pallas_call | solution.py:266
  424.4 1.3 collective-permute-start.35
  426.4 8.9 %bwd_half.37 = (bf16[6,128,1536]{2,1,0:T(8,128)(2,1)S(1)}, bf16[6,128,1536]{2,1,0:T(8,128)(2,1)S(1)}, bf16[6,128,2304]{2,1,0:T(8,128)(2,1)S(1)}, bf16[6,128,768]...) custom-call(s32[1]{0:T(128)} %bitcast.sec, ...), custom_call_target="tpu_custom_call", output_to_operand_aliasing={{0}: (6, {}), {1}: (7, {}), {2}: (8, {}), {3}: (9, {}), {4}... | custom-call | flops 2415919104 | bytes 12582912 | tf_op jit(solution)/shard_map/bwd_half/pallas_call | solution.py:266
  435.3 1.3 collective-permute-start.34
  437.3 10.1 %bwd_half.38 = (bf16[6,128,1536]{2,1,0:T(8,128)(2,1)S(1)}, bf16[6,128,1536]{2,1,0:T(8,128)(2,1)S(1)}, bf16[6,128,2304]{2,1,0:T(8,128)(2,1)S(1)}, bf16[6,128,768]...) custom-call(s32[1]{0:T(128)} %bitcast.sec, ...), custom_call_target="tpu_custom_call", output_to_operand_aliasing={{0}: (6, {}), {1}: (7, {}), {2}: (8, {}), {3}: (9, {}), {4}... | custom-call | flops 2415919104 | bytes 12582912 | tf_op jit(solution)/shard_map/bwd_half/pallas_call | solution.py:266
  447.4 9.5 %bwd_half.39 = (bf16[6,128,1536]{2,1,0:T(8,128)(2,1)S(1)}, bf16[6,128,1536]{2,1,0:T(8,128)(2,1)S(1)}, bf16[6,128,2304]{2,1,0:T(8,128)(2,1)S(1)}, bf16[6,128,768]...) custom-call(s32[1]{0:T(128)} %bitcast.sec, ...), custom_call_target="tpu_custom_call", output_to_operand_aliasing={{0}: (6, {}), {1}: (7, {}), {2}: (8, {}), {3}: (9, {}), {4}... | custom-call | flops 2415919104 | bytes 12582912 | tf_op jit(solution)/shard_map/bwd_half/pallas_call | solution.py:266
  456.9 1.8 copy-done.1
  458.7 3.5 bitcast_convert_fusion.1
  462.3 9.8 %bitcast_convert_fusion = bf16[1536,2304]{1,0:T(8,128)(2,1)} fusion(bf16[6,128,1536]{2,1,0:T(8,128)(2,1)S(1)} %get-tuple-element.623, bf16[6,128,2304]{2,1,0:T(8,128)(2,1)} %copy-done.1), kind=kOutput, calls=%fused_computation | convolution fusion | flops 5439356928 | bytes 12976128 | tf_op jit(solution)/shard_map/dot_general | solution.py:20
  472.3 1.2 collective-permute-done.36
  473.4 2.2 collective-permute-start.38
  475.6 1.8 collective-permute-start.39
  479.3 1.8 collective-permute-done.37
  481.0 2.2 collective-permute-start.40
  483.2 1.6 collective-permute-done.40
  484.8 1.2 multiply_reduce_fusion
  486.0 34.7 %reduce-scatter.5.cloned.1.call-done = bf16[48,1536]{1,0:T(8,128)(2,1)} async-done(((bf16[768,1536]{1,0:T(8,128)(2,1)}), bf16[48,1536]{1,0:T(8,128)(2,1)}) %reduce-scatter.5.cloned.1.call-update) | async-done | bytes 147472 | tf_op jit(solution)/shard_map/reduce_scatter | solution.py:392
  520.7 1.6 fusion.3
  522.3 71.2 %reduce-scatter.3.cloned.1.call-done = bf16[96,2304]{1,0:T(8,128)(2,1)} async-done(((bf16[1536,2304]{1,0:T(8,128)(2,1)}), bf16[96,2304]{1,0:T(8,128)(2,1)}) %reduce-scatter.3.cloned.1.call-update) | async-done | bytes 442384 | tf_op jit(solution)/shard_map/reduce_scatter | solution.py:393
  593.5 1.8 fusion
  598.6 4.4 collective-permute-start.43
  603.0 1.9 collective-permute-start.44
  604.9 1.7 collective-permute-done.44
  606.6 1.9 collective-permute-done.42
  609.2 2.9 collective-permute-done.45
  612.2 2.9 collective-permute-start.46
  615.0 1.6 convert_bitcast_fusion.1
  617.3 3.2 collective-permute-start.49
  621.4 2.0 convert_bitcast_fusion
  623.4 2.2 collective-permute-done.48
  (135 shorter events, 33.7 us)
Async XLA Ops:
  7.2 4.7 copy-start.6
  7.2 62.4 %all-gather.3.cloned.1.call-start = ((), (), s32[]{:S(2)}) async-start(), calls=%async_computation.4 | async-start | bytes 10027008 | tf_op jit(solution)/shard_map/all_gather | solution.py:314
  10.1 510.7 %reduce-scatter.5.cloned.1.call-start = ((), (), s32[]{:S(2)}) async-start(), calls=%async_computation.3 | async-start | bytes 2506752 | tf_op jit(solution)/shard_map/reduce_scatter | solution.py:392
  69.6 0.8 copy-start.4
  69.6 3.7 copy-start
  73.3 1.7 copy-start.2
  82.0 10.7 %collective-permute-start = (bf16[128,1536]{1,0:T(8,128)(2,1)S(1)}, bf16[128,1536]{1,0:T(8,128)(2,1)S(1)}, u32[]{:S(2)}, u32[]{:S(2)}) collective-permute-start(bf16[128,1536]{1,0:T(8,128)(2,1)S(1)} %get-tuple-element.316), channel_id=1, source_target_pairs={{0,16},{16,32},{32,48},{1,17},{17,33},{33,49},{2,18},{18,34},{34,5... | collective-permute-start | bytes 1179656 | tf_op jit(solution)/shard_map/ppermute | solution.py:374
  89.8 14.2 %collective-permute-start.2 = (bf16[128,1536]{1,0:T(8,128)(2,1)S(1)}, bf16[128,1536]{1,0:T(8,128)(2,1)S(1)}, u32[]{:S(2)}, u32[]{:S(2)}) collective-permute-start(bf16[128,1536]{1,0:T(8,128)(2,1)S(1)} %get-tuple-element.328), channel_id=1, source_target_pairs={{0,16},{16,32},{32,48},{1,17},{17,33},{33,49},{2,18},{18,34},{34,5... | collective-permute-start | bytes 1179656 | tf_op jit(solution)/shard_map/ppermute | solution.py:374
  99.6 14.2 %collective-permute-start.1 = (bf16[128,1536]{1,0:T(8,128)(2,1)S(1)}, bf16[128,1536]{1,0:T(8,128)(2,1)S(1)}, u32[]{:S(2)}, u32[]{:S(2)}) collective-permute-start(bf16[128,1536]{1,0:T(8,128)(2,1)S(1)} %get-tuple-element.327), channel_id=1, source_target_pairs={{0,16},{16,32},{32,48},{1,17},{17,33},{33,49},{2,18},{18,34},{34,5... | collective-permute-start | bytes 1179656 | tf_op jit(solution)/shard_map/ppermute | solution.py:374
  111.9 11.4 %collective-permute-start.4 = (bf16[128,1536]{1,0:T(8,128)(2,1)S(1)}, bf16[128,1536]{1,0:T(8,128)(2,1)S(1)}, u32[]{:S(2)}, u32[]{:S(2)}) collective-permute-start(bf16[128,1536]{1,0:T(8,128)(2,1)S(1)} %get-tuple-element.340), channel_id=1, source_target_pairs={{0,16},{16,32},{32,48},{1,17},{17,33},{33,49},{2,18},{18,34},{34,5... | collective-permute-start | bytes 1179656 | tf_op jit(solution)/shard_map/ppermute | solution.py:374
  120.8 11.8 %collective-permute-start.3 = (bf16[128,1536]{1,0:T(8,128)(2,1)S(1)}, bf16[128,1536]{1,0:T(8,128)(2,1)S(1)}, u32[]{:S(2)}, u32[]{:S(2)}) collective-permute-start(bf16[128,1536]{1,0:T(8,128)(2,1)S(1)} %get-tuple-element.339), channel_id=1, source_target_pairs={{0,16},{16,32},{32,48},{1,17},{17,33},{33,49},{2,18},{18,34},{34,5... | collective-permute-start | bytes 1179656 | tf_op jit(solution)/shard_map/ppermute | solution.py:374
  129.8 9.7 %collective-permute-start.6 = (bf16[128,1536]{1,0:T(8,128)(2,1)S(1)}, bf16[128,1536]{1,0:T(8,128)(2,1)S(1)}, u32[]{:S(2)}, u32[]{:S(2)}) collective-permute-start(bf16[128,1536]{1,0:T(8,128)(2,1)S(1)} %get-tuple-element.352), channel_id=1, source_target_pairs={{0,16},{16,32},{32,48},{1,17},{17,33},{33,49},{2,18},{18,34},{34,5... | collective-permute-start | bytes 1179656 | tf_op jit(solution)/shard_map/ppermute | solution.py:374
  132.7 15.1 %collective-permute-start.5 = (bf16[128,1536]{1,0:T(8,128)(2,1)S(1)}, bf16[128,1536]{1,0:T(8,128)(2,1)S(1)}, u32[]{:S(2)}, u32[]{:S(2)}) collective-permute-start(bf16[128,1536]{1,0:T(8,128)(2,1)S(1)} %get-tuple-element.351), channel_id=1, source_target_pairs={{16,32},{32,48},{48,64},{17,33},{33,49},{49,65},{18,34},{34,50},{5... | collective-permute-start | bytes 1179656 | tf_op jit(solution)/shard_map/ppermute | solution.py:374
  147.1 1.6 collective-permute-start.8
  148.0 1.6 collective-permute-start.7
  148.8 1.6 collective-permute-start.10
  149.7 9.2 %collective-permute-start.9 = (bf16[128,1536]{1,0:T(8,128)(2,1)S(1)}, bf16[128,1536]{1,0:T(8,128)(2,1)S(1)}, u32[]{:S(2)}, u32[]{:S(2)}) collective-permute-start(bf16[128,1536]{1,0:T(8,128)(2,1)S(1)} %get-tuple-element.375), channel_id=1, source_target_pairs={{48,64},{64,80},{80,96},{49,65},{65,81},{81,97},{50,66},{66,82},{8... | collective-permute-start | bytes 1179656 | tf_op jit(solution)/shard_map/ppermute | solution.py:374
  158.2 1.6 collective-permute-start.12
  159.0 1.6 collective-permute-start.11
  159.9 2.9 collective-permute-start.14
  160.6 1.7 copy-start.5
  160.7 2.3 copy-start.3
  160.7 11.1 %collective-permute-start.13 = (bf16[128,1536]{1,0:T(8,128)(2,1)S(1)}, bf16[128,1536]{1,0:T(8,128)(2,1)S(1)}, u32[]{:S(2)}, u32[]{:S(2)}) collective-permute-start(bf16[128,1536]{1,0:T(8,128)(2,1)S(1)} %get-tuple-element.399), channel_id=1, source_target_pairs={{64,80},{80,96},{96,112},{65,81},{81,97},{97,113},{66,82},{82,98},... | collective-permute-start | bytes 1179656 | tf_op jit(solution)/shard_map/ppermute | solution.py:374
  169.7 11.9 %collective-permute-start.18 = (bf16[128,1536]{1,0:T(8,128)(2,1)S(1)}, bf16[128,1536]{1,0:T(8,128)(2,1)S(1)}, u32[]{:S(2)}, u32[]{:S(2)}) collective-permute-start(bf16[128,1536]{1,0:T(8,128)(2,1)S(1)} %get-tuple-element.428), channel_id=1, source_target_pairs={{64,80},{80,96},{96,112},{65,81},{81,97},{97,113},{66,82},{82,98},... | collective-permute-start | bytes 1179656 | tf_op jit(solution)/shard_map/ppermute | solution.py:374
  171.2 10.6 %collective-permute-start.17 = (bf16[128,1536]{1,0:T(8,128)(2,1)S(1)}, bf16[128,1536]{1,0:T(8,128)(2,1)S(1)}, u32[]{:S(2)}, u32[]{:S(2)}) collective-permute-start(bf16[128,1536]{1,0:T(8,128)(2,1)S(1)} %get-tuple-element.427), channel_id=1, source_target_pairs={{80,64},{96,80},{112,96},{81,65},{97,81},{113,97},{82,66},{98,82},... | collective-permute-start | bytes 1179656 | tf_op jit(solution)/shard_map/ppermute | solution.py:386
  172.0 11.4 %collective-permute-start.16 = (bf16[128,1536]{1,0:T(8,128)(2,1)S(1)}, bf16[128,1536]{1,0:T(8,128)(2,1)S(1)}, u32[]{:S(2)}, u32[]{:S(2)}) collective-permute-start(bf16[128,1536]{1,0:T(8,128)(2,1)S(1)} %get-tuple-element.426), channel_id=1, source_target_pairs={{64,80},{80,96},{96,112},{65,81},{81,97},{97,113},{66,82},{82,98},... | collective-permute-start | bytes 1179656 | tf_op jit(solution)/shard_map/ppermute | solution.py:374
  180.9 2.6 collective-permute-start.15
  182.0 11.5 %collective-permute-start.20 = (bf16[128,1536]{1,0:T(8,128)(2,1)S(1)}, bf16[128,1536]{1,0:T(8,128)(2,1)S(1)}, u32[]{:S(2)}, u32[]{:S(2)}) collective-permute-start(bf16[128,1536]{1,0:T(8,128)(2,1)S(1)} %get-tuple-element.458), channel_id=1, source_target_pairs={{80,64},{96,80},{112,96},{81,65},{97,81},{113,97},{82,66},{98,82},... | collective-permute-start | bytes 1179656 | tf_op jit(solution)/shard_map/ppermute | solution.py:386
  182.7 10.7 %collective-permute-start.21 = (bf16[128,1536]{1,0:T(8,128)(2,1)S(1)}, bf16[128,1536]{1,0:T(8,128)(2,1)S(1)}, u32[]{:S(2)}, u32[]{:S(2)}) collective-permute-start(bf16[128,1536]{1,0:T(8,128)(2,1)S(1)} %get-tuple-element.459), channel_id=1, source_target_pairs={{64,80},{80,96},{96,112},{65,81},{81,97},{97,113},{66,82},{82,98},... | collective-permute-start | bytes 1179656 | tf_op jit(solution)/shard_map/ppermute | solution.py:374
  192.7 1.8 collective-permute-start.19
  193.8 1.6 collective-permute-start.23
  194.7 9.0 %collective-permute-start.22 = (bf16[128,1536]{1,0:T(8,128)(2,1)S(1)}, bf16[128,1536]{1,0:T(8,128)(2,1)S(1)}, u32[]{:S(2)}, u32[]{:S(2)}) collective-permute-start(bf16[128,1536]{1,0:T(8,128)(2,1)S(1)} %get-tuple-element.483), channel_id=1, source_target_pairs={{80,64},{96,80},{112,96},{81,65},{97,81},{113,97},{82,66},{98,82},... | collective-permute-start | bytes 1179656 | tf_op jit(solution)/shard_map/ppermute | solution.py:386
  202.9 1.6 collective-permute-start.25
  203.8 1.6 collective-permute-start.24
  204.7 8.6 %collective-permute-start.27 = (bf16[128,1536]{1,0:T(8,128)(2,1)S(1)}, bf16[128,1536]{1,0:T(8,128)(2,1)S(1)}, u32[]{:S(2)}, u32[]{:S(2)}) collective-permute-start(bf16[128,1536]{1,0:T(8,128)(2,1)S(1)} %get-tuple-element.524), channel_id=1, source_target_pairs={{48,32},{64,48},{80,64},{49,33},{65,49},{81,65},{50,34},{66,50},{8... | collective-permute-start | bytes 1179656 | tf_op jit(solution)/shard_map/ppermute | solution.py:386
  212.6 1.6 collective-permute-start.26
  213.5 1.6 collective-permute-start.29
  214.4 9.8 %collective-permute-start.28 = (bf16[128,1536]{1,0:T(8,128)(2,1)S(1)}, bf16[128,1536]{1,0:T(8,128)(2,1)S(1)}, u32[]{:S(2)}, u32[]{:S(2)}) collective-permute-start(bf16[128,1536]{1,0:T(8,128)(2,1)S(1)} %get-tuple-element.543), channel_id=1, source_target_pairs={{32,16},{48,32},{64,48},{33,17},{49,33},{65,49},{34,18},{50,34},{6... | collective-permute-start | bytes 1179656 | tf_op jit(solution)/shard_map/ppermute | solution.py:386
  222.9 168.0 %collective-permute-start.31 = (bf16[128,1536]{1,0:T(8,128)(2,1)S(1)}, bf16[128,1536]{1,0:T(8,128)(2,1)S(1)}, u32[]{:S(2)}, u32[]{:S(2)}) collective-permute-start(bf16[128,1536]{1,0:T(8,128)(2,1)S(1)} %get-tuple-element.564), channel_id=1, source_target_pairs={{16,0},{32,16},{48,32},{17,1},{33,17},{49,33},{18,2},{34,18},{50,3... | collective-permute-start | bytes 1179656 | tf_op jit(solution)/shard_map/ppermute | solution.py:386
  224.4 179.8 %collective-permute-start.30 = (bf16[128,1536]{1,0:T(8,128)(2,1)S(1)}, bf16[128,1536]{1,0:T(8,128)(2,1)S(1)}, u32[]{:S(2)}, u32[]{:S(2)}) collective-permute-start(bf16[128,1536]{1,0:T(8,128)(2,1)S(1)} %get-tuple-element.563), channel_id=1, source_target_pairs={{16,0},{32,16},{48,32},{17,1},{33,17},{49,33},{18,2},{34,18},{50,3... | collective-permute-start | bytes 1179656 | tf_op jit(solution)/shard_map/ppermute | solution.py:386
  399.9 15.6 %collective-permute-start.33 = (bf16[128,1536]{1,0:T(8,128)(2,1)S(1)}, bf16[128,1536]{1,0:T(8,128)(2,1)S(1)}, u32[]{:S(2)}, u32[]{:S(2)}) collective-permute-start(bf16[128,1536]{1,0:T(8,128)(2,1)S(1)} %get-tuple-element.584), channel_id=1, source_target_pairs={{16,0},{32,16},{48,32},{17,1},{33,17},{49,33},{18,2},{34,18},{50,3... | collective-permute-start | bytes 1179656 | tf_op jit(solution)/shard_map/ppermute | solution.py:386
  413.4 13.0 %collective-permute-start.32 = (bf16[128,1536]{1,0:T(8,128)(2,1)S(1)}, bf16[128,1536]{1,0:T(8,128)(2,1)S(1)}, u32[]{:S(2)}, u32[]{:S(2)}) collective-permute-start(bf16[128,1536]{1,0:T(8,128)(2,1)S(1)} %get-tuple-element.583), channel_id=1, source_target_pairs={{16,0},{32,16},{48,32},{17,1},{33,17},{49,33},{18,2},{34,18},{50,3... | collective-permute-start | bytes 1179656 | tf_op jit(solution)/shard_map/ppermute | solution.py:386
  424.4 12.9 %collective-permute-start.35 = (bf16[128,1536]{1,0:T(8,128)(2,1)S(1)}, bf16[128,1536]{1,0:T(8,128)(2,1)S(1)}, u32[]{:S(2)}, u32[]{:S(2)}) collective-permute-start(bf16[128,1536]{1,0:T(8,128)(2,1)S(1)} %get-tuple-element.604), channel_id=1, source_target_pairs={{16,0},{32,16},{48,32},{17,1},{33,17},{49,33},{18,2},{34,18},{50,3... | collective-permute-start | bytes 1179656 | tf_op jit(solution)/shard_map/ppermute | solution.py:386
  435.3 12.1 %collective-permute-start.34 = (bf16[128,1536]{1,0:T(8,128)(2,1)S(1)}, bf16[128,1536]{1,0:T(8,128)(2,1)S(1)}, u32[]{:S(2)}, u32[]{:S(2)}) collective-permute-start(bf16[128,1536]{1,0:T(8,128)(2,1)S(1)} %get-tuple-element.603), channel_id=1, source_target_pairs={{16,0},{32,16},{48,32},{17,1},{33,17},{49,33},{18,2},{34,18},{50,3... | collective-permute-start | bytes 1179656 | tf_op jit(solution)/shard_map/ppermute | solution.py:386
  456.9 1.8 copy-start.1
  462.3 131.3 %reduce-scatter.3.cloned.1.call-start = ((), (), s32[]{:S(2)}) async-start(), calls=%async_computation.2 | async-start | bytes 7520256 | tf_op jit(solution)/shard_map/reduce_scatter | solution.py:393
  472.2 1.3 collective-permute-start.36
  473.4 5.2 collective-permute-start.38
  475.6 3.7 collective-permute-start.39
  477.4 3.7 collective-permute-start.37
  481.0 3.8 collective-permute-start.40
  597.3 1.2 collective-permute-start.41
  598.6 6.4 %collective-permute-start.43 = (f32[8,128]{1,0:T(8,128)S(1)}, f32[8,128]{1,0:T(8,128)S(1)}, u32[]{:S(2)}, u32[]{:S(2)}) collective-permute-start(f32[8,128]{1,0:T(8,128)S(1)} %broadcast_add_fusion), channel_id=1, source_target_pairs={{0,4},{1,5},{2,6},{3,7},{4,0},{5,1},{6,2},{7,3},{8,12},{9,13},{10,... | collective-permute-start | bytes 12296 | tf_op jit(solution)/shard_map/ppermute | solution.py:294
  603.0 3.6 collective-permute-start.44
  604.9 3.6 collective-permute-start.42
  608.6 3.6 collective-permute-start.45
  612.2 5.1 collective-permute-start.46
  617.3 6.1 collective-permute-start.49
  620.4 5.1 collective-permute-start.48
  620.9 4.6 collective-permute-start.47
Sparse Core Ops, SparseCore 0:
  10.3 59.2 all-gather.2
  462.4 58.3 reduce-scatter.4
  523.2 70.3 reduce-scatter.2

commit v3 on v2

v3 whole, which is shorter than its diff:
```python
import functools
import math

import jax
import jax.numpy as jnp
from jax import lax
from jax.experimental import pallas as pl
from jax.experimental.pallas import tpu as pltpu
from jax.sharding import PartitionSpec as P

HEAD = 128
ROWS = 64
EPS = 1e-05
MASKED = -1e30
MOST = 128
LIMIT = 8 * 1024 * 1024
BF = jnp.bfloat16
F32 = jnp.float32


def mm(left, right, lc=1, rc=0):
    return lax.dot_general(left, right, (((lc,), (rc,)), ((), ())), preferred_element_type=F32)


def unit(h):
    r = lax.rsqrt(jnp.mean(h * h, axis=-1, keepdims=True) + EPS)
    return r, h * r


def w_in(pack, k, inner):
    return pack[:, :, k * inner:(k + 1) * inner].reshape(-1, inner)


def w_out(pack, part, inner):
    half = pack.shape[1] // 2
    return pack[:, part * half:(part + 1) * half, 3 * inner:].reshape(-1, inner)


def prepare_kernel(cotangent, scale, *refs):
    seeds, sq, acc = refs[-3:]
    seeds[...] = (cotangent[...].astype(F32) * scale[0]).astype(BF)
    sq[...] = jnp.zeros_like(sq)
    acc[...] = jnp.zeros_like(acc)


def forward_kernel(cycle, micro, last, sec, recv, hid, bias, gains, pack, *refs):
    (sh, sa, sq, so, sl, out) = refs[5:11]
    inner = so.shape[2]
    heads = inner // HEAD
    span = bias.shape[2]
    section = sec[0]
    m = cycle - 2 * section

    @pl.when((m >= 0) & (m < micro))
    def _():
        own = pl.multiple_of(m * ROWS, ROWS)
        base = pl.multiple_of(own + span - ROWS, ROWS)
        h = jnp.where(section == 0, hid[pl.ds(own, ROWS)], recv[...])
        sh[m] = h
        _, u = unit(h.astype(F32))
        a = (u * gains[...]).astype(BF)
        sa[m] = a
        for k in range(3):
            sq[pl.ds(base, ROWS), k * inner:(k + 1) * inner] = mm(a, w_in(pack, k, inner)).astype(BF)
        mask = bias[m]
        scores = []
        for e in range(heads):
            lo, hi = e * HEAD, (e + 1) * HEAD
            q = sq[pl.ds(base, ROWS), lo:hi]
            k = sq[pl.ds(own, span), inner + lo:inner + hi]
            scores.append(mm(q, k, 1, 1) * HEAD ** (-0.5) + mask)
        tops = [jnp.max(s, axis=-1, keepdims=True) for s in scores]
        xs = [jnp.exp(s - top) for s, top in zip(scores, tops)]
        totals = [jnp.sum(x, axis=-1, keepdims=True) for x in xs]
        lane = lax.broadcasted_iota(jnp.int32, (ROWS, HEAD), 1)
        lse = jnp.zeros((ROWS, HEAD), F32)
        for e in range(heads):
            lo, hi = e * HEAD, (e + 1) * HEAD
            v = sq[pl.ds(own, span), 2 * inner + lo:2 * inner + hi]
            so[m, :, lo:hi] = (mm(xs[e].astype(BF), v) * (1.0 / totals[e])).astype(BF)
            lse = jnp.where(lane == e, tops[e] + jnp.log(totals[e]), lse)
        sl[m] = lse

        @pl.when(section != last)
        def _():
            o = so[m]
            for part in range(2):
                cols = slice(part * inner, (part + 1) * inner)
                out[:, cols] = (
                    sh[m, :, cols].astype(F32) + mm(o, w_out(pack, part, inner))
                ).astype(BF)


def backward_kernel(cycle, first, micro, last, per, sec, recv, seeds, bias, gains, pack, *refs):
    (sh, sa, sq, so, sl, sg, sd, sn, acc, out) = refs[9:19]
    inner = so.shape[2]
    feat = sh.shape[2]
    heads = inner // HEAD
    span = bias.shape[2]
    section = sec[0]
    n = cycle - first - 2 * (last - section)

    @pl.when((n >= 0) & (n < micro))
    def _():
        m = (n // per) * per + (per - 1) - n % per
        own = pl.multiple_of(m * ROWS, ROWS)
        base = pl.multiple_of(own + span - ROWS, ROWS)
        g = jnp.where(section == last, seeds[pl.ds(own, ROWS)], recv[...])
        sg[m] = g
        do_all = (
            mm(g[:, :inner], w_out(pack, 0, inner), 1, 1)
            + mm(g[:, inner:], w_out(pack, 1, inner), 1, 1)
        ).astype(BF)
        mask = bias[m]
        lse = sl[m]
        scale = HEAD ** (-0.5)
        cut = [slice(e * HEAD, (e + 1) * HEAD) for e in range(heads)]
        qs = [sq[pl.ds(base, ROWS), e * HEAD:(e + 1) * HEAD] for e in range(heads)]
        ks = [sq[pl.ds(own, span), inner + e * HEAD:inner + (e + 1) * HEAD] for e in range(heads)]
        vs = [sq[pl.ds(own, span), 2 * inner + e * HEAD:2 * inner + (e + 1) * HEAD] for e in range(heads)]
        dos = [do_all[:, c] for c in cut]
        ps = [jnp.exp(mm(qs[e], ks[e], 1, 1) * scale + mask - lse[:, e:e + 1]) for e in range(heads)]
        dps = [mm(dos[e], vs[e], 1, 1) for e in range(heads)]
        insides = [jnp.sum(dp * p, axis=-1, keepdims=True) for dp, p in zip(dps, ps)]
        dss = [(p * (dp - i) * scale).astype(BF) for p, dp, i in zip(ps, dps, insides)]
        for e in range(heads):
            lo, hi = e * HEAD, (e + 1) * HEAD
            sd[m, :, lo:hi] = mm(dss[e], ks[e]).astype(BF)
            dk = mm(dss[e], qs[e], 0, 0)
            dv = mm(ps[e].astype(BF), dos[e], 0, 0)
            for at, value in ((0, dk), (inner, dv)):
                total = acc[pl.ds(own, span), at + lo:at + hi] + value
                acc[pl.ds(own, span - ROWS), at + lo:at + hi] = total[:span - ROWS]
                sd[m, :, inner + at + lo:inner + at + hi] = total[span - ROWS:].astype(BF)
        r, u = unit(sh[m].astype(F32))
        da = None
        for k in range(3):
            term = mm(sd[m, :, k * inner:(k + 1) * inner], w_in(pack, k, inner), 1, 1)
            da = term if da is None else da + term
        sn[m] = jnp.sum((da * u).reshape(ROWS // 8, 8, feat), axis=0)
        e = da * gains[...]
        mean = jnp.mean(e * u, axis=-1, keepdims=True)
        out[...] = (sg[m].astype(F32) + r * (e - u * mean)).astype(BF)


SMEM = pl.BlockSpec(memory_space=pltpu.SMEM)
VMEM = pl.BlockSpec(memory_space=pltpu.VMEM)


def call(body, ins, states, out_shape, flops, name):
    count = len(ins)
    shapes = [jax.ShapeDtypeStruct(s.shape, s.dtype) for s in states]
    got = pl.pallas_call(
        body,
        out_shape=shapes + [out_shape],
        in_specs=[SMEM] + [VMEM] * (count - 1 + len(states)),
        out_specs=[VMEM] * (len(states) + 1),
        input_output_aliases={count + i: i for i in range(len(states))},
        compiler_params=pltpu.CompilerParams(vmem_limit_bytes=LIMIT),
        cost_estimate=pl.CostEstimate(flops=flops, bytes_accessed=12 * 1024 * 1024, transcendentals=0),
        name=name,
    )(*ins, *states)
    return got[-1], list(got[:-1])


def pair_set(on, low, high, size):
    hops = [s for s in on if low <= s < high]
    if not hops:
        return []
    size = max(size, len(hops))
    start = min(max(hops[-1] - size + 1, low), high - size)
    return list(range(start, start + size))


def spread_sum(value, whole):
    rounds = [[1], [2, 4, 6], [8]]
    if whole:
        rounds = [[1], [2, 4, 6], [8], [64], [16, 32, 48]]
    for masks in rounds:
        got = [
            lax.ppermute(value, ("section", "dp"), [(i, i ^ mask) for i in range(128)])
            for mask in masks
        ]
        for other in got:
            value = value + other
    return value


def local(hidden_in, segment_ids, cotangent, in_proj, out_proj, norm_gains):
    section = lax.axis_index("section")
    sections = lax.axis_size("section")
    width = lax.axis_size("dp")
    last = sections - 1
    seqs, length = segment_ids.shape
    feat = hidden_in.shape[1]
    shard = in_proj.shape[1]
    inner = out_proj.shape[1] * width
    micro = seqs * length // ROWS
    wo = jnp.concatenate([out_proj[0, :, :inner], out_proj[0, :, inner:]], axis=0)
    pack = lax.all_gather(jnp.concatenate([in_proj[0], wo], axis=1), "dp", axis=0)
    loss_scale = 1.0 / math.sqrt(width * hidden_in.shape[0])
    per = length // ROWS
    window = min(per, MOST // ROWS + 1)
    span = window * ROWS
    ahead = span - ROWS
    tokens = seqs * length
    ident = segment_ids + 8 * lax.broadcasted_iota(jnp.int32, (seqs, length), 0)
    ident = ident.reshape(micro, ROWS)
    padded = jnp.concatenate([jnp.full((ahead,), -1, jnp.int32), ident.reshape(tokens)])
    keys = jnp.stack([padded[i * ROWS:i * ROWS + span] for i in range(micro)])
    rows = lax.broadcasted_iota(jnp.int32, (ROWS, span), 0) + ahead
    cols = lax.broadcasted_iota(jnp.int32, (ROWS, span), 1)
    allowed = (cols <= rows)[None] & (ident[:, :, None] == keys[:, None, :])
    bias = jnp.where(allowed, 0.0, MASKED).astype(F32)
    sec = jnp.full((1,), section, jnp.int32)

    def shaped(*shape, dtype=BF):
        return jax.ShapeDtypeStruct(shape, dtype)

    sh, sa, so, sl, sg, sd, sn, seeds, sq, acc = pl.pallas_call(
        prepare_kernel,
        out_shape=[
            shaped(micro, ROWS, feat),
            shaped(micro, ROWS, feat),
            shaped(micro, ROWS, inner),
            shaped(micro, ROWS, HEAD, dtype=F32),
            shaped(micro, ROWS, feat),
            shaped(micro, ROWS, 3 * inner),
            shaped(micro, 8, feat, dtype=F32),
            shaped(tokens, feat),
            shaped(tokens + ahead, 3 * inner),
            shaped(tokens + ahead, 2 * inner, dtype=F32),
        ],
        in_specs=[VMEM, SMEM],
        out_specs=[VMEM] * 10,
        compiler_params=pltpu.CompilerParams(vmem_limit_bytes=LIMIT),
        cost_estimate=pl.CostEstimate(flops=10**9, bytes_accessed=40 * 1024 * 1024, transcendentals=0),
        name="prepare",
    )(cotangent, jnp.full((1,), loss_scale, F32))
    states = [sh, sa, sq, so, sl, sg, sd, sn, acc]
    moved = jax.ShapeDtypeStruct((ROWS, feat), BF)
    per_row = 2 * feat * 4 * inner
    first = 2 * last + per - 1
    end = first + 2 * last + micro
    gains = norm_gains
    f_recv, b_recv = {}, {}
    for cycle in range(end):
        on = [s for s in range(sections) if 0 <= cycle - 2 * s < micro]
        if on:
            out, states[:5] = call(
                functools.partial(forward_kernel, cycle, micro, last),
                [sec, f_recv.get(cycle, hidden_in[:ROWS]), hidden_in, bias, gains, pack],
                states[:5], moved, ROWS * per_row, "fwd_half",
            )
            pairs = pair_set(on, 0, last, micro // 2)
            if pairs:
                pairs = [(s, s + 1) for s in pairs]
                f_recv[cycle + 2] = lax.ppermute(out, "section", pairs)
        on = [s for s in range(sections) if 0 <= cycle - first - 2 * (last - s) < micro]
        if on:
            out, states = call(
                functools.partial(backward_kernel, cycle, first, micro, last, per),
                [sec, b_recv.get(cycle, seeds[:ROWS]), seeds, bias, gains, pack],
                states, moved, 2 * ROWS * per_row, "bwd_half",
            )
            pairs = pair_set([s - 1 for s in on], 0, last, micro // 2 if cycle > first + 3 else 1)
            if pairs:
                pairs = [(s + 1, s) for s in pairs]
                b_recv[cycle + 2] = lax.ppermute(out, "section", pairs)
    sa, so, sg, sd, sn = states[1], states[3], states[5], states[6], states[7]
    out_part = mm(so.reshape(tokens, inner), sg.reshape(tokens, feat), 0, 0).astype(BF)
    in_part = mm(sa.reshape(tokens, feat), sd.reshape(tokens, 3 * inner), 0, 0).astype(BF)
    gain_part = jnp.sum(sn, axis=(0, 1)).astype(BF).astype(F32).reshape(feat // HEAD, HEAD)
    out_sum = lax.psum_scatter(out_part, "dp", scatter_dimension=0, tiled=True).astype(F32)
    in_sum = lax.psum_scatter(in_part, "dp", scatter_dimension=0, tiled=True).astype(F32)
    gain_all = spread_sum(gain_part, False).reshape(feat)
    own = feat // width
    gain_sum = lax.dynamic_slice_in_dim(gain_all, lax.axis_index("dp") * own, own)
    squares = jnp.sum(in_sum * in_sum) + jnp.sum(out_sum * out_sum) + jnp.sum(gain_sum * gain_sum)
    grand_total = spread_sum(jnp.full((8, HEAD), squares, F32), True)[0, 0]
    count = float(sections * width * (in_sum.size + out_sum.size + gain_sum.size))
    return (in_sum[None], out_sum[None], gain_sum[None], jnp.sqrt(grand_total / count))


def solution(mesh):
    placed = (
        P("dp", None),
        P("dp", None),
        P("dp", None),
        P("section", "dp", None),
        P("section", "dp", None),
        P("section", None),
    )
    return jax.shard_map(
        local,
        mesh=mesh,
        in_specs=placed,
        out_specs=(P("section", "dp", None), P("section", "dp", None), P("section", "dp"), P()),
        check_vma=False,
    )
```

time: 644 us -> 586 us (0.910)
  waiting for transfers between devices: 358 us -> 292 us
  Pallas kernels: 163 us -> 99 us
  local copies, waits for them, and re-layouts: 11.7 us -> 48.2 us
  starting transfers between devices: 59.7 us -> 90.9 us
    pallas_call x40 -> x53, Pallas kernels: 163 us -> 99 us  [the longest x52 98 us: call(): pl.pallas_call(body, out_shape=shapes + [out_shape], in_specs=[SMEM] + [V...]
    ppermute x18 -> x24, waiting for transfers between devices: 170 us -> 127 us  [local(): b_recv[cycle + 2] = lax.ppermute(out, 'section', pairs)]
    unnamed x14 -> x80, local copies, waits for them, and re-layouts: 7.3 us -> 43.7 us
    ppermute x18 -> x24, starting transfers between devices: 22.5 us -> 47.6 us  [local(): f_recv[cycle + 2] = lax.ppermute(out, 'section', pairs)]
    all_gather x1, waiting for transfers between devices: 57.5 us -> 39.8 us  [local(): lax.all_gather(jnp.concatenate([in_proj[0], wo], axis=1), 'dp', axis=0)]
    ppermute x18 -> x24, starting transfers between devices: 16 us -> 23.7 us  [local(): b_recv[cycle + 2] = lax.ppermute(out, 'section', pairs)]
  transfers between devices with their start and end apart: 53 -> 65, of which waited for: 21 -> 29; matrix products, arithmetic and copies ran while one was open for 3% -> 4% of each run, Pallas kernels for 23% -> 16%
where the time goes in v3:
time: 586 us; the launch traced here: 575 us
  waiting for transfers between devices  292 us (50%)
  Pallas kernels  99 us (17%)
  starting transfers between devices  90.9 us (16%)
  local copies, waits for them, and re-layouts  48.2 us (8%)
  between operations  19.1 us (3%)
  matrix products  13.2 us (2%)
  other arithmetic  12.2 us (2%)
    ppermute x24, waiting for transfers between devices, local(): b_recv[cycle + 2] = lax.ppermute(out, 'section', pairs)  127 us
    pallas_call x52, Pallas kernels, call(): pl.pallas_call(body, out_shape=shapes + [out_shape], in_specs=[SMEM] + [V...  98 us
    reduce_scatter x1, waiting for transfers between devices, local(): lax.psum_scatter(in_part, 'dp', scatter_dimension=0, tiled=True).astype(F32)  71.1 us
    ppermute x24, starting transfers between devices, local(): f_recv[cycle + 2] = lax.ppermute(out, 'section', pairs)  47.6 us
    unnamed x80, local copies, waits for them, and re-layouts  43.7 us
    all_gather x1, waiting for transfers between devices, local(): lax.all_gather(jnp.concatenate([in_proj[0], wo], axis=1), 'dp', axis=0)  39.8 us
    reduce_scatter x1, waiting for transfers between devices, local(): lax.psum_scatter(out_part, 'dp', scatter_dimension=0, tiled=True)  35 us
    ppermute x24, starting transfers between devices, local(): b_recv[cycle + 2] = lax.ppermute(out, 'section', pairs)  23.7 us
  transfers between devices with their start and end apart: 65, of which 29 were waited for; matrix products, arithmetic and copies ran while one was open for 4% of the time, Pallas kernels for 16%

profile of v3, /device:TPU:2, one launch (start us, length us, event | category | flops | bytes accessed | tf_op | source)
XLA Modules:
  0.0 574.8 jit_solution(13637646700074845686)
XLA Ops:
  19.9 2.4 copy-done.11
  29.8 39.8 %all-gather.3.cloned.1.call-done = bf16[1536,3072]{1,0:T(8,128)(2,1)} async-done(((bf16[96,3072]{1,0:T(8,128)(2,1)}), bf16[1536,3072]{1,0:T(8,128)(2,1)}) %all-gather.3.cloned.1.call-update) | async-done | bytes 9437200 | tf_op jit(solution)/shard_map/all_gather | solution.py:200
  69.5 3.7 copy-done
  73.2 2.2 copy-done.2
  81.8 2.7 fwd_half.26
  85.8 2.7 fwd_half.27
  90.6 2.7 fwd_half.28
  93.3 4.4 collective-permute-start.1
  97.7 2.7 fwd_half.29
  102.4 2.7 fwd_half.30
  105.1 3.8 collective-permute-start.3
  108.9 3.0 fwd_half.31
  111.9 3.5 collective-permute-start.6
  115.5 2.7 fwd_half.32
  120.1 2.7 fwd_half.33
  122.8 3.9 collective-permute-start.8
  126.7 2.7 fwd_half.34
  129.4 4.3 collective-permute-start.7
  133.7 2.7 fwd_half.35
  136.4 3.8 collective-permute-start.10
  140.2 2.7 fwd_half.36
  145.1 2.7 fwd_half.37
  147.8 7.0 %collective-permute-start.12 = (bf16[64,1536]{1,0:T(8,128)(2,1)S(1)}, bf16[64,1536]{1,0:T(8,128)(2,1)S(1)}, u32[]{:S(2)}, u32[]{:S(2)}) collective-permute-start(bf16[64,1536]{1,0:T(8,128)(2,1)S(1)} %get-tuple-element.500), channel_id=1, source_target_pairs={{0,16},{16,32},{32,48},{48,64},{64,80},{80,96},{1,17},{17,33},{33,... | collective-permute-start | bytes 589832 | tf_op jit(solution)/shard_map/ppermute | solution.py:258
  155.7 2.3 collective-permute-done.12.recv
  166.0 2.1 copy-done.3
  170.3 2.2 copy-done.4
  177.0 4.5 fwd_half.46
  185.8 3.6 fwd_half.49
  192.8 4.3 bwd_half.34
  200.0 5.1 bwd_half.38
  207.7 92.8 %collective-permute-done.37.recv = bf16[64,1536]{1,0:T(8,128)(2,1)S(1)} collective-permute-done((bf16[64,1536]{1,0:T(8,128)(2,1)S(1)}, bf16[64,1536]{1,0:T(8,128)(2,1)S(1)}, u32[]{:S(2)}, u32[]{:S(2)}) %collective-permute-start.37) | collective-permute-done | bytes 196640 | tf_op jit(solution)/shard_map/ppermute | solution.py:269
  300.5 3.6 bwd_half.40
  305.5 7.9 %collective-permute-done.36.recv = bf16[64,1536]{1,0:T(8,128)(2,1)S(1)} collective-permute-done((bf16[64,1536]{1,0:T(8,128)(2,1)S(1)}, bf16[64,1536]{1,0:T(8,128)(2,1)S(1)}, u32[]{:S(2)}, u32[]{:S(2)}) %collective-permute-start.36) | collective-permute-done | bytes 196640 | tf_op jit(solution)/shard_map/ppermute | solution.py:269
  313.3 3.6 bwd_half.41
  318.3 2.7 collective-permute-done.39.recv
  321.0 3.8 bwd_half.42
  326.1 4.0 collective-permute-done.38.recv
  330.1 3.6 bwd_half.43
  336.1 3.6 bwd_half.44
  341.1 2.9 collective-permute-done.40.recv
  344.0 3.6 bwd_half.45
  350.0 3.8 bwd_half.46
  355.1 3.4 collective-permute-done.42.recv
  358.5 3.6 bwd_half.47
  364.6 3.6 bwd_half.48
  369.6 4.9 collective-permute-done.44.recv
  374.5 3.6 bwd_half.49
  381.2 4.6 bwd_half.50
  385.7 3.3 collective-permute-done.46.recv
  389.0 4.3 bwd_half.51
  397.4 3.4 bitcast_convert_fusion.1
  402.5 9.8 %bitcast_convert_fusion = bf16[1536,2304]{1,0:T(8,128)(2,1)} fusion(bf16[12,64,1536]{2,1,0:T(8,128)(2,1)S(1)} %copy-done.10, bf16[12,64,2304]{2,1,0:T(8,128)(2,1)} %copy-done.14), kind=kOutput, calls=%fused_computation | convolution fusion | flops 5439356928 | bytes 12976128 | tf_op jit(solution)/shard_map/dot_general | solution.py:22
  416.6 2.7 collective-permute-start.49
  421.7 2.9 collective-permute-done.52
  425.8 35.0 %reduce-scatter.5.cloned.1.call-done = bf16[48,1536]{1,0:T(8,128)(2,1)} async-done(((bf16[768,1536]{1,0:T(8,128)(2,1)}), bf16[48,1536]{1,0:T(8,128)(2,1)}) %reduce-scatter.5.cloned.1.call-update) | async-done | bytes 147472 | tf_op jit(solution)/shard_map/reduce_scatter | solution.py:274
  462.4 71.1 %reduce-scatter.3.cloned.1.call-done = bf16[96,2304]{1,0:T(8,128)(2,1)} async-done(((bf16[1536,2304]{1,0:T(8,128)(2,1)}), bf16[96,2304]{1,0:T(8,128)(2,1)}) %reduce-scatter.3.cloned.1.call-update) | async-done | bytes 442384 | tf_op jit(solution)/shard_map/reduce_scatter | solution.py:275
  538.6 4.4 collective-permute-start.55
  542.9 2.0 collective-permute-start.56
  546.5 2.0 collective-permute-done.54
  549.2 2.9 collective-permute-done.57
  552.1 2.7 collective-permute-start.58
  557.3 3.1 collective-permute-start.61
  561.4 2.0 convert_bitcast_fusion
  563.3 2.2 collective-permute-done.60
  (236 shorter events, 106.6 us)
Async XLA Ops:
  7.2 62.3 %all-gather.3.cloned.1.call-start = ((), (), s32[]{:S(2)}) async-start(), calls=%async_computation.4 | async-start | bytes 10027008 | tf_op jit(solution)/shard_map/all_gather | solution.py:200
  10.1 450.8 %reduce-scatter.5.cloned.1.call-start = ((), (), s32[]{:S(2)}) async-start(), calls=%async_computation.3 | async-start | bytes 2506752 | tf_op jit(solution)/shard_map/reduce_scatter | solution.py:274
  84.5 6.1 %collective-permute-start = (bf16[64,1536]{1,0:T(8,128)(2,1)S(1)}, bf16[64,1536]{1,0:T(8,128)(2,1)S(1)}, u32[]{:S(2)}, u32[]{:S(2)}) collective-permute-start(bf16[64,1536]{1,0:T(8,128)(2,1)S(1)} %get-tuple-element.428), channel_id=1, source_target_pairs={{0,16},{16,32},{32,48},{48,64},{64,80},{80,96},{1,17},{17,33},{33,... | collective-permute-start | bytes 589832 | tf_op jit(solution)/shard_map/ppermute | solution.py:258
  88.5 9.2 %collective-permute-start.2 = (bf16[64,1536]{1,0:T(8,128)(2,1)S(1)}, bf16[64,1536]{1,0:T(8,128)(2,1)S(1)}, u32[]{:S(2)}, u32[]{:S(2)}) collective-permute-start(bf16[64,1536]{1,0:T(8,128)(2,1)S(1)} %get-tuple-element.440), channel_id=1, source_target_pairs={{0,16},{16,32},{32,48},{48,64},{64,80},{80,96},{1,17},{17,33},{33,... | collective-permute-start | bytes 589832 | tf_op jit(solution)/shard_map/ppermute | solution.py:258
  93.3 9.0 %collective-permute-start.1 = (bf16[64,1536]{1,0:T(8,128)(2,1)S(1)}, bf16[64,1536]{1,0:T(8,128)(2,1)S(1)}, u32[]{:S(2)}, u32[]{:S(2)}) collective-permute-start(bf16[64,1536]{1,0:T(8,128)(2,1)S(1)} %get-tuple-element.439), channel_id=1, source_target_pairs={{0,16},{16,32},{32,48},{48,64},{64,80},{80,96},{1,17},{17,33},{33,... | collective-permute-start | bytes 589832 | tf_op jit(solution)/shard_map/ppermute | solution.py:258
  100.4 8.4 %collective-permute-start.4 = (bf16[64,1536]{1,0:T(8,128)(2,1)S(1)}, bf16[64,1536]{1,0:T(8,128)(2,1)S(1)}, u32[]{:S(2)}, u32[]{:S(2)}) collective-permute-start(bf16[64,1536]{1,0:T(8,128)(2,1)S(1)} %get-tuple-element.452), channel_id=1, source_target_pairs={{0,16},{16,32},{32,48},{48,64},{64,80},{80,96},{1,17},{17,33},{33,... | collective-permute-start | bytes 589832 | tf_op jit(solution)/shard_map/ppermute | solution.py:258
  105.1 10.4 %collective-permute-start.3 = (bf16[64,1536]{1,0:T(8,128)(2,1)S(1)}, bf16[64,1536]{1,0:T(8,128)(2,1)S(1)}, u32[]{:S(2)}, u32[]{:S(2)}) collective-permute-start(bf16[64,1536]{1,0:T(8,128)(2,1)S(1)} %get-tuple-element.451), channel_id=1, source_target_pairs={{0,16},{16,32},{32,48},{48,64},{64,80},{80,96},{1,17},{17,33},{33,... | collective-permute-start | bytes 589832 | tf_op jit(solution)/shard_map/ppermute | solution.py:258
  111.9 8.2 %collective-permute-start.6 = (bf16[64,1536]{1,0:T(8,128)(2,1)S(1)}, bf16[64,1536]{1,0:T(8,128)(2,1)S(1)}, u32[]{:S(2)}, u32[]{:S(2)}) collective-permute-start(bf16[64,1536]{1,0:T(8,128)(2,1)S(1)} %get-tuple-element.464), channel_id=1, source_target_pairs={{0,16},{16,32},{32,48},{48,64},{64,80},{80,96},{1,17},{17,33},{33,... | collective-permute-start | bytes 589832 | tf_op jit(solution)/shard_map/ppermute | solution.py:258
  118.2 8.5 %collective-permute-start.5 = (bf16[64,1536]{1,0:T(8,128)(2,1)S(1)}, bf16[64,1536]{1,0:T(8,128)(2,1)S(1)}, u32[]{:S(2)}, u32[]{:S(2)}) collective-permute-start(bf16[64,1536]{1,0:T(8,128)(2,1)S(1)} %get-tuple-element.463), channel_id=1, source_target_pairs={{0,16},{16,32},{32,48},{48,64},{64,80},{80,96},{1,17},{17,33},{33,... | collective-permute-start | bytes 589832 | tf_op jit(solution)/shard_map/ppermute | solution.py:258
  122.8 10.9 %collective-permute-start.8 = (bf16[64,1536]{1,0:T(8,128)(2,1)S(1)}, bf16[64,1536]{1,0:T(8,128)(2,1)S(1)}, u32[]{:S(2)}, u32[]{:S(2)}) collective-permute-start(bf16[64,1536]{1,0:T(8,128)(2,1)S(1)} %get-tuple-element.476), channel_id=1, source_target_pairs={{0,16},{16,32},{32,48},{48,64},{64,80},{80,96},{1,17},{17,33},{33,... | collective-permute-start | bytes 589832 | tf_op jit(solution)/shard_map/ppermute | solution.py:258
  129.4 10.8 %collective-permute-start.7 = (bf16[64,1536]{1,0:T(8,128)(2,1)S(1)}, bf16[64,1536]{1,0:T(8,128)(2,1)S(1)}, u32[]{:S(2)}, u32[]{:S(2)}) collective-permute-start(bf16[64,1536]{1,0:T(8,128)(2,1)S(1)} %get-tuple-element.475), channel_id=1, source_target_pairs={{0,16},{16,32},{32,48},{48,64},{64,80},{80,96},{1,17},{17,33},{33,... | collective-permute-start | bytes 589832 | tf_op jit(solution)/shard_map/ppermute | solution.py:258
  136.4 8.7 %collective-permute-start.10 = (bf16[64,1536]{1,0:T(8,128)(2,1)S(1)}, bf16[64,1536]{1,0:T(8,128)(2,1)S(1)}, u32[]{:S(2)}, u32[]{:S(2)}) collective-permute-start(bf16[64,1536]{1,0:T(8,128)(2,1)S(1)} %get-tuple-element.488), channel_id=1, source_target_pairs={{0,16},{16,32},{32,48},{48,64},{64,80},{80,96},{1,17},{17,33},{33,... | collective-permute-start | bytes 589832 | tf_op jit(solution)/shard_map/ppermute | solution.py:258
  142.9 11.9 %collective-permute-start.9 = (bf16[64,1536]{1,0:T(8,128)(2,1)S(1)}, bf16[64,1536]{1,0:T(8,128)(2,1)S(1)}, u32[]{:S(2)}, u32[]{:S(2)}) collective-permute-start(bf16[64,1536]{1,0:T(8,128)(2,1)S(1)} %get-tuple-element.487), channel_id=1, source_target_pairs={{0,16},{16,32},{32,48},{48,64},{64,80},{80,96},{1,17},{17,33},{33,... | collective-permute-start | bytes 589832 | tf_op jit(solution)/shard_map/ppermute | solution.py:258
  147.8 10.2 %collective-permute-start.12 = (bf16[64,1536]{1,0:T(8,128)(2,1)S(1)}, bf16[64,1536]{1,0:T(8,128)(2,1)S(1)}, u32[]{:S(2)}, u32[]{:S(2)}) collective-permute-start(bf16[64,1536]{1,0:T(8,128)(2,1)S(1)} %get-tuple-element.500), channel_id=1, source_target_pairs={{0,16},{16,32},{32,48},{48,64},{64,80},{80,96},{1,17},{17,33},{33,... | collective-permute-start | bytes 589832 | tf_op jit(solution)/shard_map/ppermute | solution.py:258
  155.0 3.6 collective-permute-start.11
  158.0 1.4 collective-permute-start.14
  158.7 1.5 collective-permute-start.13
  159.4 3.9 collective-permute-start.16
  162.4 11.0 %collective-permute-start.15 = (bf16[64,1536]{1,0:T(8,128)(2,1)S(1)}, bf16[64,1536]{1,0:T(8,128)(2,1)S(1)}, u32[]{:S(2)}, u32[]{:S(2)}) collective-permute-start(bf16[64,1536]{1,0:T(8,128)(2,1)S(1)} %get-tuple-element.523), channel_id=1, source_target_pairs={{16,32},{32,48},{48,64},{64,80},{80,96},{96,112},{17,33},{33,49},{... | collective-permute-start | bytes 589832 | tf_op jit(solution)/shard_map/ppermute | solution.py:258
  168.1 7.4 %collective-permute-start.20 = (bf16[64,1536]{1,0:T(8,128)(2,1)S(1)}, bf16[64,1536]{1,0:T(8,128)(2,1)S(1)}, u32[]{:S(2)}, u32[]{:S(2)}) collective-permute-start(bf16[64,1536]{1,0:T(8,128)(2,1)S(1)} %get-tuple-element.556), channel_id=1, source_target_pairs={{16,32},{32,48},{48,64},{64,80},{80,96},{96,112},{17,33},{33,49},{... | collective-permute-start | bytes 589832 | tf_op jit(solution)/shard_map/ppermute | solution.py:258
  172.7 3.6 collective-permute-start.19
  174.1 2.8 collective-permute-start.18
  174.8 7.3 %collective-permute-start.17 = (bf16[64,1536]{1,0:T(8,128)(2,1)S(1)}, bf16[64,1536]{1,0:T(8,128)(2,1)S(1)}, u32[]{:S(2)}, u32[]{:S(2)}) collective-permute-start(bf16[64,1536]{1,0:T(8,128)(2,1)S(1)} %get-tuple-element.553), channel_id=1, source_target_pairs={{112,96},{113,97},{114,98},{115,99},{116,100},{117,101},{118,102},... | collective-permute-start | bytes 589832 | tf_op jit(solution)/shard_map/ppermute | solution.py:269
  175.5 7.3 %collective-permute-start.24 = (bf16[64,1536]{1,0:T(8,128)(2,1)S(1)}, bf16[64,1536]{1,0:T(8,128)(2,1)S(1)}, u32[]{:S(2)}, u32[]{:S(2)}) collective-permute-start(bf16[64,1536]{1,0:T(8,128)(2,1)S(1)} %get-tuple-element.588), channel_id=1, source_target_pairs={{16,32},{32,48},{48,64},{64,80},{80,96},{96,112},{17,33},{33,49},{... | collective-permute-start | bytes 589832 | tf_op jit(solution)/shard_map/ppermute | solution.py:258
  176.3 7.3 %collective-permute-start.23 = (bf16[64,1536]{1,0:T(8,128)(2,1)S(1)}, bf16[64,1536]{1,0:T(8,128)(2,1)S(1)}, u32[]{:S(2)}, u32[]{:S(2)}) collective-permute-start(bf16[64,1536]{1,0:T(8,128)(2,1)S(1)} %get-tuple-element.587), channel_id=1, source_target_pairs={{96,80},{112,96},{97,81},{113,97},{98,82},{114,98},{99,83},{115,99... | collective-permute-start | bytes 589832 | tf_op jit(solution)/shard_map/ppermute | solution.py:269
  181.5 2.8 collective-permute-start.22
  182.2 2.8 collective-permute-start.21
  182.9 2.8 collective-permute-start.28
  183.6 5.7 collective-permute-start.27
  184.3 6.4 %collective-permute-start.26 = (bf16[64,1536]{1,0:T(8,128)(2,1)S(1)}, bf16[64,1536]{1,0:T(8,128)(2,1)S(1)}, u32[]{:S(2)}, u32[]{:S(2)}) collective-permute-start(bf16[64,1536]{1,0:T(8,128)(2,1)S(1)} %get-tuple-element.618), channel_id=1, source_target_pairs={{16,32},{32,48},{48,64},{64,80},{80,96},{96,112},{17,33},{33,49},{... | collective-permute-start | bytes 589832 | tf_op jit(solution)/shard_map/ppermute | solution.py:258
  185.1 6.4 %collective-permute-start.25 = (bf16[64,1536]{1,0:T(8,128)(2,1)S(1)}, bf16[64,1536]{1,0:T(8,128)(2,1)S(1)}, u32[]{:S(2)}, u32[]{:S(2)}) collective-permute-start(bf16[64,1536]{1,0:T(8,128)(2,1)S(1)} %get-tuple-element.617), channel_id=1, source_target_pairs={{32,16},{48,32},{64,48},{80,64},{96,80},{112,96},{33,17},{49,33},{... | collective-permute-start | bytes 589832 | tf_op jit(solution)/shard_map/ppermute | solution.py:269
  189.4 3.5 collective-permute-start.30
  190.1 2.1 collective-permute-start.31
  191.4 6.3 %collective-permute-start.29 = (bf16[64,1536]{1,0:T(8,128)(2,1)S(1)}, bf16[64,1536]{1,0:T(8,128)(2,1)S(1)}, u32[]{:S(2)}, u32[]{:S(2)}) collective-permute-start(bf16[64,1536]{1,0:T(8,128)(2,1)S(1)} %get-tuple-element.649), channel_id=1, source_target_pairs={{32,16},{48,32},{64,48},{80,64},{96,80},{112,96},{33,17},{49,33},{... | collective-permute-start | bytes 589832 | tf_op jit(solution)/shard_map/ppermute | solution.py:269
  197.1 1.4 collective-permute-start.33
  197.8 1.4 collective-permute-start.32
  198.5 1.4 collective-permute-start.35
  199.3 7.1 %collective-permute-start.34 = (bf16[64,1536]{1,0:T(8,128)(2,1)S(1)}, bf16[64,1536]{1,0:T(8,128)(2,1)S(1)}, u32[]{:S(2)}, u32[]{:S(2)}) collective-permute-start(bf16[64,1536]{1,0:T(8,128)(2,1)S(1)} %get-tuple-element.695), channel_id=1, source_target_pairs={{32,16},{48,32},{64,48},{80,64},{96,80},{112,96},{33,17},{49,33},{... | collective-permute-start | bytes 589832 | tf_op jit(solution)/shard_map/ppermute | solution.py:269
  205.1 95.4 %collective-permute-start.37 = (bf16[64,1536]{1,0:T(8,128)(2,1)S(1)}, bf16[64,1536]{1,0:T(8,128)(2,1)S(1)}, u32[]{:S(2)}, u32[]{:S(2)}) collective-permute-start(bf16[64,1536]{1,0:T(8,128)(2,1)S(1)} %get-tuple-element.716), channel_id=1, source_target_pairs={{16,0},{32,16},{48,32},{64,48},{80,64},{96,80},{17,1},{33,17},{49,... | collective-permute-start | bytes 589832 | tf_op jit(solution)/shard_map/ppermute | solution.py:269
  206.4 106.9 %collective-permute-start.36 = (bf16[64,1536]{1,0:T(8,128)(2,1)S(1)}, bf16[64,1536]{1,0:T(8,128)(2,1)S(1)}, u32[]{:S(2)}, u32[]{:S(2)}) collective-permute-start(bf16[64,1536]{1,0:T(8,128)(2,1)S(1)} %get-tuple-element.715), channel_id=1, source_target_pairs={{16,0},{32,16},{48,32},{64,48},{80,64},{96,80},{17,1},{33,17},{49,... | collective-permute-start | bytes 589832 | tf_op jit(solution)/shard_map/ppermute | solution.py:269
  304.2 16.8 %collective-permute-start.39 = (bf16[64,1536]{1,0:T(8,128)(2,1)S(1)}, bf16[64,1536]{1,0:T(8,128)(2,1)S(1)}, u32[]{:S(2)}, u32[]{:S(2)}) collective-permute-start(bf16[64,1536]{1,0:T(8,128)(2,1)S(1)} %get-tuple-element.736), channel_id=1, source_target_pairs={{16,0},{32,16},{48,32},{64,48},{80,64},{96,80},{17,1},{33,17},{49,... | collective-permute-start | bytes 589832 | tf_op jit(solution)/shard_map/ppermute | solution.py:269
  317.0 13.2 %collective-permute-start.38 = (bf16[64,1536]{1,0:T(8,128)(2,1)S(1)}, bf16[64,1536]{1,0:T(8,128)(2,1)S(1)}, u32[]{:S(2)}, u32[]{:S(2)}) collective-permute-start(bf16[64,1536]{1,0:T(8,128)(2,1)S(1)} %get-tuple-element.735), channel_id=1, source_target_pairs={{16,0},{32,16},{48,32},{64,48},{80,64},{96,80},{17,1},{33,17},{49,... | collective-permute-start | bytes 589832 | tf_op jit(solution)/shard_map/ppermute | solution.py:269
  324.8 11.3 %collective-permute-start.41 = (bf16[64,1536]{1,0:T(8,128)(2,1)S(1)}, bf16[64,1536]{1,0:T(8,128)(2,1)S(1)}, u32[]{:S(2)}, u32[]{:S(2)}) collective-permute-start(bf16[64,1536]{1,0:T(8,128)(2,1)S(1)} %get-tuple-element.756), channel_id=1, source_target_pairs={{16,0},{32,16},{48,32},{64,48},{80,64},{96,80},{17,1},{33,17},{49,... | collective-permute-start | bytes 589832 | tf_op jit(solution)/shard_map/ppermute | solution.py:269
  333.8 10.2 %collective-permute-start.40 = (bf16[64,1536]{1,0:T(8,128)(2,1)S(1)}, bf16[64,1536]{1,0:T(8,128)(2,1)S(1)}, u32[]{:S(2)}, u32[]{:S(2)}) collective-permute-start(bf16[64,1536]{1,0:T(8,128)(2,1)S(1)} %get-tuple-element.755), channel_id=1, source_target_pairs={{16,0},{32,16},{48,32},{64,48},{80,64},{96,80},{17,1},{33,17},{49,... | collective-permute-start | bytes 589832 | tf_op jit(solution)/shard_map/ppermute | solution.py:269
  339.8 10.2 %collective-permute-start.43 = (bf16[64,1536]{1,0:T(8,128)(2,1)S(1)}, bf16[64,1536]{1,0:T(8,128)(2,1)S(1)}, u32[]{:S(2)}, u32[]{:S(2)}) collective-permute-start(bf16[64,1536]{1,0:T(8,128)(2,1)S(1)} %get-tuple-element.776), channel_id=1, source_target_pairs={{16,0},{32,16},{48,32},{64,48},{80,64},{96,80},{17,1},{33,17},{49,... | collective-permute-start | bytes 589832 | tf_op jit(solution)/shard_map/ppermute | solution.py:269
  347.7 10.8 %collective-permute-start.42 = (bf16[64,1536]{1,0:T(8,128)(2,1)S(1)}, bf16[64,1536]{1,0:T(8,128)(2,1)S(1)}, u32[]{:S(2)}, u32[]{:S(2)}) collective-permute-start(bf16[64,1536]{1,0:T(8,128)(2,1)S(1)} %get-tuple-element.775), channel_id=1, source_target_pairs={{16,0},{32,16},{48,32},{64,48},{80,64},{96,80},{17,1},{33,17},{49,... | collective-permute-start | bytes 589832 | tf_op jit(solution)/shard_map/ppermute | solution.py:269
  353.8 10.8 %collective-permute-start.45 = (bf16[64,1536]{1,0:T(8,128)(2,1)S(1)}, bf16[64,1536]{1,0:T(8,128)(2,1)S(1)}, u32[]{:S(2)}, u32[]{:S(2)}) collective-permute-start(bf16[64,1536]{1,0:T(8,128)(2,1)S(1)} %get-tuple-element.796), channel_id=1, source_target_pairs={{16,0},{32,16},{48,32},{64,48},{80,64},{96,80},{17,1},{33,17},{49,... | collective-permute-start | bytes 589832 | tf_op jit(solution)/shard_map/ppermute | solution.py:269
  362.1 12.3 %collective-permute-start.44 = (bf16[64,1536]{1,0:T(8,128)(2,1)S(1)}, bf16[64,1536]{1,0:T(8,128)(2,1)S(1)}, u32[]{:S(2)}, u32[]{:S(2)}) collective-permute-start(bf16[64,1536]{1,0:T(8,128)(2,1)S(1)} %get-tuple-element.795), channel_id=1, source_target_pairs={{16,0},{32,16},{48,32},{64,48},{80,64},{96,80},{17,1},{33,17},{49,... | collective-permute-start | bytes 589832 | tf_op jit(solution)/shard_map/ppermute | solution.py:269
  368.3 12.9 %collective-permute-start.47 = (bf16[64,1536]{1,0:T(8,128)(2,1)S(1)}, bf16[64,1536]{1,0:T(8,128)(2,1)S(1)}, u32[]{:S(2)}, u32[]{:S(2)}) collective-permute-start(bf16[64,1536]{1,0:T(8,128)(2,1)S(1)} %get-tuple-element.816), channel_id=1, source_target_pairs={{16,0},{32,16},{48,32},{64,48},{80,64},{96,80},{17,1},{33,17},{49,... | collective-permute-start | bytes 589832 | tf_op jit(solution)/shard_map/ppermute | solution.py:269
  378.1 10.9 %collective-permute-start.46 = (bf16[64,1536]{1,0:T(8,128)(2,1)S(1)}, bf16[64,1536]{1,0:T(8,128)(2,1)S(1)}, u32[]{:S(2)}, u32[]{:S(2)}) collective-permute-start(bf16[64,1536]{1,0:T(8,128)(2,1)S(1)} %get-tuple-element.815), channel_id=1, source_target_pairs={{16,0},{32,16},{48,32},{64,48},{80,64},{96,80},{17,1},{33,17},{49,... | collective-permute-start | bytes 589832 | tf_op jit(solution)/shard_map/ppermute | solution.py:269
  400.8 132.7 %reduce-scatter.3.cloned.1.call-start = ((), (), s32[]{:S(2)}) async-start(), calls=%async_computation.2 | async-start | bytes 7520256 | tf_op jit(solution)/shard_map/reduce_scatter | solution.py:275
  413.4 1.2 collective-permute-start.48
  414.6 5.3 collective-permute-start.50
  416.4 3.7 collective-permute-start.51
  416.6 4.3 collective-permute-start.49
  421.0 3.7 collective-permute-start.52
  538.6 6.4 %collective-permute-start.55 = (f32[8,128]{1,0:T(8,128)S(1)}, f32[8,128]{1,0:T(8,128)S(1)}, u32[]{:S(2)}, u32[]{:S(2)}) collective-permute-start(f32[8,128]{1,0:T(8,128)S(1)} %broadcast_add_fusion), channel_id=1, source_target_pairs={{0,4},{1,5},{2,6},{3,7},{4,0},{5,1},{6,2},{7,3},{8,12},{9,13},{10,... | collective-permute-start | bytes 12296 | tf_op jit(solution)/shard_map/ppermute | solution.py:181
  542.9 3.6 collective-permute-start.56
  544.9 3.6 collective-permute-start.54
  548.5 3.6 collective-permute-start.57
  552.1 5.1 collective-permute-start.58
  557.3 6.1 %collective-permute-start.61 = (f32[8,128]{1,0:T(8,128)S(1)}, f32[8,128]{1,0:T(8,128)S(1)}, u32[]{:S(2)}, u32[]{:S(2)}) collective-permute-start(f32[8,128]{1,0:T(8,128)S(1)} %add.83), channel_id=1, source_target_pairs={{0,48},{1,49},{2,50},{3,51},{4,52},{5,53},{6,54},{7,55},{8,56},{9,... | collective-permute-start | bytes 12296 | tf_op jit(solution)/shard_map/ppermute | solution.py:181
  560.4 5.1 collective-permute-start.60
  561.1 4.4 collective-permute-start.59
  (41 other events, 167.2 us)
Sparse Core Ops, SparseCore 0:
  10.2 59.2 all-gather.2
  400.9 59.8 reduce-scatter.4
  463.3 70.1 reduce-scatter.2
